TPU v7x, 256 devices: a whole 4x4x8 slice. The times are simulated.
256 devices in a mesh: seq: 64 (over x, z_lo, y), tp: 4 (over z_hi, core).
Axes of the slice: x: 4, y: 4, z: 8 (z_hi: 2, z_lo: 4; z = z_hi * 4 + z_lo), core: 2. Of those that a mesh axis runs over, the one named last changes fastest.
Arguments:
- latents: float32 [256, 256, 1152], P('tp', 'seq'), may hold values from -100 to 100
- time_embed: float32 [256, 1152], P('seq'), may hold values from -3 to 3
- modulation: float32 [3, 3, 1152], replicated, may hold values from -2 to 2
- qkv_weight: bfloat16 [2, 1152, 3, 1152], P(None, None, None, 'tp'), may hold values from -6 to 6
- out_weight: bfloat16 [2, 1152, 1152], P(None, 'tp'), may hold values from -0.1875 to 0.1875
- mlp_in_weight: bfloat16 [1152, 4608], P(None, 'tp'), may hold values from -0.1875 to 0.1875
- mlp_out_weight: bfloat16 [4608, 1152], P('tp'), may hold values from -0.09375 to 0.09375
Outputs:
- result: float32 [256, 256, 1152], P('tp', 'seq')
All inputs are finite; a program needn't handle non-finite values.
Results may differ from a plain program's by a relative error of at most 0.0045.
Values may be sent and summed in bfloat16 or wider, within the bound.
No kernel may reach another device: no remote copies, remote signals or barrier semaphores. Data moves between devices by JAX's collectives and lax.ppermute only.
A program may use at most 128 MiB of HBM per device.

v0:
```python
import functools
import math

import jax
import jax.numpy as jnp
from jax import lax
from jax.experimental import pallas as pl
from jax.experimental.pallas import tpu as pltpu
from jax.sharding import PartitionSpec as P

HD = 72
BF = jnp.bfloat16
F32 = jnp.float32
PLANE = [[x * 16 + z * 4 + y for x in range(4) for y in range(4)] for z in range(4)]
SWAPS = {d: [(t, t ^ d) for t in range(4)] for d in (1, 2, 3)}


def dot(a, b, ca, cb):
    return lax.dot_general(a, b, (((ca,), (cb,)), ((), ())), preferred_element_type=F32)


def attend_kernel(pieces, ready, layer, *refs):
    x_refs, refs = refs[:pieces], refs[pieces:]
    inits, refs = refs[:ready], refs[ready:]
    out_refs, (held, sems, stage, out_sems, came) = refs[-pieces - 5 : -5], refs[-5:]
    sources = refs[: -pieces - 5]
    heads = 4
    width = heads * HD
    length = 256
    plan = []
    if len(sources) == 4:
        for k in range(2):
            plan.append((sources[2 * k].at[layer], held.at[k, pl.ds(0, 3 * width)]))
            plan.append((sources[2 * k + 1].at[layer], held.at[k, pl.ds(3 * width, width)]))
    else:
        for k in range(2):
            plan.append((sources[k], held.at[k]))
    wide = pieces == 1
    items = 1 if wide else 2
    arrivals = []
    if not wide:
        part = stage.shape[1] // items
        for d, ref in enumerate(x_refs):
            rows = ref.at[pl.ds(0, items * part)]
            arrivals.append(pltpu.make_async_copy(rows, came.at[d], out_sems.at[d]))
            arrivals[-1].start()
    copies = [pltpu.make_async_copy(a, b, sems.at[i]) for i, (a, b) in enumerate(plan)]
    each = len(copies) // 2
    for copy in copies[:each]:
        copy.start()
    model = held.shape[2]
    if wide:
        part = x_refs[0].shape[0]
        spans = [slice(j * model, (j + 1) * model) for j in range(length // part)]
        x = jnp.concatenate([x_refs[0][:, span] for span in spans], axis=0)
    else:
        for arrival in arrivals:
            arrival.wait()
        spans = [slice(s * part, (s + 1) * part) for s in range(items)]
        x = jnp.concatenate([came[d, span] for span in spans for d in range(pieces)], axis=0)

    def shard(k):
        for copy in copies[each * k : each * (k + 1)]:
            copy.wait()
        for copy in copies[each * (k + 1) : each * (k + 2)]:
            copy.start()
        packed = dot(held[k, : 3 * width, :], x, 1, 1)
        columns = []
        for s in range(items):
            item = packed[:, s * length : (s + 1) * length]
            mixed = []
            for h in range(heads):
                q = item[h * HD : (h + 1) * HD] * (math.log2(math.e) / math.sqrt(HD))
                kk = item[width + h * HD : width + (h + 1) * HD]
                v = item[2 * width + h * HD : 2 * width + (h + 1) * HD].astype(BF)
                qh = q.astype(BF).astype(F32)
                kh = kk.astype(BF).astype(F32)
                left = jnp.concatenate([kh, kh, kk - kh], axis=0).astype(BF)
                right = jnp.concatenate([qh, q - qh, qh], axis=0).astype(BF)
                scores = dot(left, right, 0, 0)
                top = jnp.max(scores, axis=0, keepdims=True)
                weights = jnp.exp2(scores - top)
                total = jnp.sum(weights, axis=0, keepdims=True)
                mixed.append(dot(v, weights.astype(BF), 1, 0) / total)
            columns.append(jnp.concatenate(mixed, axis=0).astype(BF))
        return dot(jnp.concatenate(columns, axis=1), held[k, 3 * width :, :], 0, 0)

    total = shard(0) + shard(1)
    if ready:
        total = total + inits[0][...]
    total = total.astype(out_refs[0].dtype)
    if not wide:
        sends = []
        for d in reversed(range(pieces)):
            for s in range(items):
                start = s * length + d * part
                stage[d, s * part : (s + 1) * part] = total[start : start + part]
            sends.append(pltpu.make_async_copy(stage.at[d], out_refs[d], out_sems.at[d]))
            sends[-1].start()
        for send in sends:
            send.wait()
    elif ready:
        for j, span in enumerate(spans):
            out_refs[0][:, span] = total[j * part : (j + 1) * part]
    else:
        out_refs[0][...] = total


def attend(layer, parts, weights, inits=()):
    width = weights[0].shape[-1]
    pieces = len(parts)
    vmem = pl.BlockSpec(memory_space=pltpu.VMEM)
    free = pl.BlockSpec(memory_space=pl.ANY)
    hbm = pl.BlockSpec(memory_space=pltpu.HBM)
    rows = parts[0].size * pieces // width
    limit = 62 if pieces > 1 else 24 if inits else 48
    outs = [jax.ShapeDtypeStruct(parts[0].shape, BF)] * pieces
    if pieces == 1 and not inits:
        outs = [jax.ShapeDtypeStruct((rows, width), F32)]
    return pl.pallas_call(
        functools.partial(attend_kernel, pieces, len(inits), layer),
        out_shape=outs,
        in_specs=[vmem if pieces == 1 else free] * pieces
        + [vmem] * len(inits)
        + [free] * len(weights),
        out_specs=[vmem if pieces == 1 else hbm] * pieces,
        scratch_shapes=[
            pltpu.VMEM((2, width, width), BF),
            pltpu.SemaphoreType.DMA((len(weights),)),
            pltpu.VMEM((pieces, *parts[0].shape) if pieces > 1 else (1, 16, 128), BF),
            pltpu.SemaphoreType.DMA((pieces,)),
            pltpu.VMEM((pieces, *parts[0].shape) if pieces > 1 else (1, 16, 128), BF),
        ],
        compiler_params=pltpu.CompilerParams(vmem_limit_bytes=limit * 2**20),
        cost_estimate=pl.CostEstimate(
            flops=6 * rows * width * width,
            bytes_accessed=4 * width * width,
            transcendentals=0,
        ),
    )(*parts, *inits, *weights)


def norm_rows(x, mod_ref, b):
    average = jnp.mean(x, axis=-1, keepdims=True)
    centred = x - average
    spread = jnp.mean(centred * centred, axis=-1, keepdims=True)
    scaled = centred * lax.rsqrt(spread + 1e-06)
    return (scaled * (1.0 + mod_ref[b, 1:2, :]) + mod_ref[b, 0:1, :]).astype(BF)


def enter_kernel(core_ref, lat_ref, mod_ref, piece_ref, keep_ref, give_ref, send_ref):
    low = core_ref[0] == 0
    part = lat_ref.shape[0]
    rows = [norm_rows(lat_ref[:, f, :], mod_ref, 0) for f in range(4)]
    for i in range(2):
        span = slice(i * part, (i + 1) * part)
        keep = jnp.where(low, rows[i], rows[2 + i])
        keep_ref[span] = keep
        send_ref[span] = keep
        give_ref[span] = jnp.where(low, rows[2 + i], rows[i])
    send_ref[2 * part :] = piece_ref[...]


def enter_spatial(core, latents, modulation, piece):
    local, _, width = latents.shape
    vmem = pl.BlockSpec(memory_space=pltpu.VMEM)
    half = jax.ShapeDtypeStruct((2 * local, width), BF)
    return pl.pallas_call(
        enter_kernel,
        out_shape=[half, half, jax.ShapeDtypeStruct((2 * local + piece.shape[0], width), BF)],
        in_specs=[pl.BlockSpec(memory_space=pltpu.SMEM)] + [vmem] * 3,
        out_specs=[vmem] * 3,
        compiler_params=pltpu.CompilerParams(vmem_limit_bytes=62 * 2**20),
    )(core.reshape(1), latents, modulation, piece)


def middle_kernel(core_ref, embed_ref, mod_ref, *refs):
    sources, (mid_ref, norm_ref), held, sems = refs[:5], refs[5:7], refs[7:12], refs[12]
    copies = [
        pltpu.make_async_copy(a, b, sems.at[i]) for i, (a, b) in enumerate(zip(sources, held))
    ]
    for copy in copies:
        copy.start()
    for copy in copies:
        copy.wait()
    lat_ref, b0, b1, b2, b3 = held
    part, _, model = lat_ref.shape
    low = core_ref[0] == 0
    for f in range(4):
        span = slice((f % 2) * part, (f % 2 + 1) * part)
        mine = b0[span].astype(F32) + b2[span].astype(F32)
        theirs = b1[span].astype(F32) + b3[span].astype(F32)
        added = jnp.where(low, mine, theirs) if f < 2 else jnp.where(low, theirs, mine)
        x = lat_ref[:, f, :] + mod_ref[0, 2:3, :] * added + embed_ref[f : f + 1, :]
        mid_ref[f] = x
        norm_ref[:, f * model : (f + 1) * model] = norm_rows(x, mod_ref, 1)


def finish_spatial(core, latents, time_embed, modulation, back):
    local, frames, width = latents.shape
    vmem = pl.BlockSpec(memory_space=pltpu.VMEM)
    return pl.pallas_call(
        middle_kernel,
        out_shape=[
            jax.ShapeDtypeStruct((frames, local, width), F32),
            jax.ShapeDtypeStruct((local, frames * width), BF),
        ],
        in_specs=[pl.BlockSpec(memory_space=pltpu.SMEM)]
        + [vmem] * 2
        + [pl.BlockSpec(memory_space=pl.ANY)] * 5,
        out_specs=[vmem] * 2,
        scratch_shapes=[pltpu.VMEM(latents.shape, F32)]
        + [pltpu.VMEM(part.shape, BF) for part in back]
        + [pltpu.SemaphoreType.DMA((5,))],
        compiler_params=pltpu.CompilerParams(vmem_limit_bytes=62 * 2**20),
    )(core.reshape(1), time_embed, modulation, latents, *back)


def mlp_kernel(first, count, mod_ref, in_a, in_b, *refs):
    sources, refs = refs[:count], refs[count:]
    outs, (held, sems, held_a, held_b, in_sems) = refs[:-5], refs[-5:]
    width = held.shape[2]
    blocks = []
    for ref in sources:
        for part in range(ref.shape[0] // width):
            blocks.append(ref.at[pl.ds(part * width, width)])
    arrivals = [
        pltpu.make_async_copy(in_a, held_a, in_sems.at[0]),
        pltpu.make_async_copy(in_b, held_b, in_sems.at[1]),
    ]
    copies = [pltpu.make_async_copy(b, held.at[i], sems.at[i]) for i, b in enumerate(blocks)]
    for copy in arrivals + copies[:2]:
        copy.start()
    arrivals[0].wait()
    if first:
        arrivals[1].wait()
        base_ref, x_ref = outs
        local = held_b.shape[0]
        for f in range(held_a.shape[0]):
            arrived = held_b[:, f * width : (f + 1) * width].astype(F32)
            hidden = held_a[f] + mod_ref[1, 2:3, :] * arrived
            base_ref[f * local : (f + 1) * local] = hidden
            x_ref[f * local : (f + 1) * local] = norm_rows(hidden, mod_ref, 2)
    else:
        x_ref, base_ref = held_a, held_b
    x = x_ref[...]
    total = None
    for k in range(0, len(blocks), 2):
        copies[k].wait()
        if k + 2 < len(blocks):
            copies[k + 2].start()
        v = dot(x, held[k], 1, 0)
        inner = 0.5 * v * (1.0 + jnp.tanh(math.sqrt(2.0 / math.pi) * (v + 0.044715 * (v * v * v))))
        copies[k + 1].wait()
        if k + 3 < len(blocks):
            copies[k + 3].start()
        part = dot(inner.astype(BF), held[k + 1], 1, 0)
        total = part if total is None else total + part
    if first:
        base_ref[...] = base_ref[...] + mod_ref[2, 2:3, :] * total
    else:
        arrivals[1].wait()
        total = base_ref[...] + mod_ref[2, 2:3, :] * total
        out_ref = outs[0]
        local, frames = out_ref.shape[:2]
        for f in range(frames):
            out_ref[:, f, :] = total[f * local : (f + 1) * local]


def mlp(first, modulation, inputs, early, late, outs):
    weights = (*early, *late)
    width = weights[0].shape[1]
    blocks = sum(w.shape[0] for w in weights) // width
    vmem = pl.BlockSpec(memory_space=pltpu.VMEM)
    limit = 48 if first else 24
    return pl.pallas_call(
        functools.partial(mlp_kernel, first, len(weights)),
        out_shape=outs,
        in_specs=[vmem] + [pl.BlockSpec(memory_space=pl.ANY)] * (2 + len(weights)),
        out_specs=[vmem] * len(outs),
        scratch_shapes=[
            pltpu.VMEM((blocks, width, width), BF),
            pltpu.SemaphoreType.DMA((blocks,)),
            pltpu.VMEM(inputs[0].shape, inputs[0].dtype),
            pltpu.VMEM(inputs[1].shape, inputs[1].dtype),
            pltpu.SemaphoreType.DMA((2,)),
        ],
        compiler_params=pltpu.CompilerParams(vmem_limit_bytes=limit * 2**20),
        cost_estimate=pl.CostEstimate(
            flops=512 * width * width * blocks,
            bytes_accessed=2 * blocks * width * width,
            transcendentals=0,
        ),
    )(modulation, *inputs, *weights)


def swap(x, d):
    return lax.ppermute(x, "tp", SWAPS[d])


def gather(piece):
    return lax.all_gather(piece, "seq", axis=0, tiled=True, axis_index_groups=PLANE)


def no_work(*refs):
    del refs


def after(x, *others):
    return pl.pallas_call(
        no_work,
        out_shape=jax.ShapeDtypeStruct(x.shape, x.dtype),
        in_specs=[pl.BlockSpec(memory_space=pl.ANY)] * (1 + len(others)),
        out_specs=pl.BlockSpec(memory_space=pl.ANY),
        input_output_aliases={0: 0},
    )(x, *others)


def on_device(
    latents, time_embed, modulation, qkv_weight, out_weight, mlp_in_weight, mlp_out_weight
):
    width = latents.shape[2]
    seq = lax.axis_index("seq")
    tp = lax.axis_index("tp")
    place = (seq // 16) * 4 + seq % 4
    core = tp % 2

    qkv = qkv_weight.transpose(0, 2, 3, 1).reshape(2, -1, width)
    other_qkv = swap(qkv, 1)
    other_out = swap(out_weight, 1)
    near = (qkv, out_weight, other_qkv, other_out)

    cut = width // 16
    piece_t = jnp.where(
        place < 12,
        lax.dynamic_slice(qkv, (1, place * cut, 0), (1, cut, width))[0],
        lax.dynamic_slice(out_weight, (1, (place - 12) * cut, 0), (1, cut, width))[0],
    )
    keep, give, send = enter_spatial(core, latents, modulation, piece_t)
    give = after(give, other_qkv, other_out)
    parts = [keep, swap(give, 1), swap(send, 2), swap(give, 3)]
    far_t = gather(after(parts[2][2 * latents.shape[0] :], parts[1], parts[3]))

    cut = width // 8
    piece_f = jnp.where(
        place < 8,
        lax.dynamic_slice_in_dim(mlp_in_weight, place * cut, cut, axis=0),
        lax.dynamic_slice_in_dim(mlp_out_weight, (place - 8) * cut, cut, axis=0),
    )
    moved = swap(piece_f, 2)
    back = attend(0, parts, near)
    back = [(back[0] if d == 0 else swap(back[d], d)) for d in range(4)]
    far_f = gather(after(moved, *back[1:]))
    middle, normed = finish_spatial(core, latents, time_embed, modulation, back)
    other_mlp_in = swap(mlp_in_weight, 1)
    other_mlp_out = swap(mlp_out_weight, 1)

    def regroup(rows):
        rows = rows.reshape(latents.shape)
        rows = lax.all_to_all(rows, "seq", split_axis=0, concat_axis=0, tiled=True)
        return rows.reshape(rows.shape[0], -1)

    regrouped = after(regroup(normed), other_mlp_in, other_mlp_out)
    partial = attend(1, [regrouped], near)
    far_t = after(far_t, regrouped)
    far_other_t = swap(far_t, 1)
    (projected,) = attend(1, [regrouped], (far_t, far_other_t), partial)
    projected = regroup(projected)
    far_f = after(far_f, projected)
    far_other_f = swap(far_f, 1)
    rows = latents.shape[0] * latents.shape[1]
    base = jax.ShapeDtypeStruct((rows, width), F32)
    x = jax.ShapeDtypeStruct((rows, width), BF)
    early = (mlp_in_weight, mlp_out_weight, other_mlp_in, other_mlp_out)
    base, x = mlp(True, modulation, (middle, projected), early, (far_f,), [base, x])
    result = jax.ShapeDtypeStruct(latents.shape, F32)
    return mlp(False, modulation, (x, base), (), (far_other_f,), [result])[0]


def solution(mesh):
    in_specs = (
        P("tp", "seq", None),
        P("seq", None),
        P(),
        P(None, None, None, "tp"),
        P(None, "tp", None),
        P(None, "tp"),
        P("tp", None),
    )
    out_specs = P("tp", "seq", None)
    return jax.shard_map(
        on_device, mesh=mesh, in_specs=in_specs, out_specs=out_specs, check_vma=False
    )
```

profile of v0, /device:TPU:1, one launch (start us, length us, event | category | flops | bytes accessed | tf_op | source)
XLA Modules:
  0.0 203.1 jit_solution(4042201897318609808)
XLA Ops:
  6.5 3.2 %collective-permute-start = (bf16[2,864,1152]{2,1,0:T(8,128)(2,1)}, bf16[2,864,1152]{2,1,0:T(8,128)(2,1)}, u32[]{:S(2)}, u32[]{:S(2)}) collective-permute-start(bf16[2,864,1152]{2,1,0:T(8,128)(2,1)} %bitcast.13), channel_id=1, source_target_pairs={{0,1},{1,0},{2,3},{3,2},{4,5},{5,4},{6,7},{7,6},{8,9},{9,8},{10,11... | collective-permute-start | bytes 11943944 | tf_op jit(solution)/shard_map/ppermute | solution.py:298
  9.8 1.7 select_bitcast_fusion.piece_ref
  11.5 2.9 %shard_map.73 = (bf16[128,1152]{1,0:T(8,128)(2,1)}, bf16[128,1152]{1,0:T(8,128)(2,1)}, bf16[200,1152]{1,0:T(8,128)(2,1)}) custom-call(s32[1]{0:T(128)} %bitcast.core_ref, f32[64,4,1152]{2,1,0:T(4,128)} %refs_0_.2, f32[3,3,1152]{2,1,0:T(4,128)} %mod_ref.7, bf16[72,1152]{1,0:T(8,128)(2,1)} %select_bitcast_fusion.piece_ref), custom_call_target="tpu_custom_call" | custom-call | tf_op jit(solution)/shard_map/pallas_call | solution.py:168
  14.4 5.2 %collective-permute-start.3 = (bf16[200,1152]{1,0:T(8,128)(2,1)}, bf16[200,1152]{1,0:T(8,128)(2,1)S(1)}, u32[]{:S(2)}, u32[]{:S(2)}) collective-permute-start(bf16[200,1152]{1,0:T(8,128)(2,1)} %get-tuple-element.18), channel_id=1, source_target_pairs={{0,2},{1,3},{2,0},{3,1},{4,6},{5,7},{6,4},{7,5},{8,10},{9,11},{10,... | collective-permute-start | bytes 1382408 | tf_op jit(solution)/shard_map/ppermute | solution.py:298
  19.6 0.0 collective-permute-done.1.refs_2_.refs_7_.refs_4_
  19.6 0.0 collective-permute-done.refs_1_.refs_6_.refs_3_
  19.6 1.1 copy-done.3
  20.7 0.8 collective-permute-start.2
  21.4 3.5 %collective-permute-start.4 = (bf16[128,1152]{1,0:T(8,128)(2,1)}, bf16[128,1152]{1,0:T(8,128)(2,1)S(1)}, u32[]{:S(2)}, u32[]{:S(2)}) collective-permute-start(bf16[128,1152]{1,0:T(8,128)(2,1)} %shard_map.74), channel_id=1, source_target_pairs={{0,3},{1,2},{2,1},{3,0},{4,7},{5,6},{6,5},{7,4},{8,11},{9,10},{10,... | collective-permute-start | bytes 884744 | tf_op jit(solution)/shard_map/ppermute | solution.py:298
  24.9 7.4 %collective-permute-done.3.refs_2_ = bf16[200,1152]{1,0:T(8,128)(2,1)S(1)} collective-permute-done((bf16[200,1152]{1,0:T(8,128)(2,1)}, bf16[200,1152]{1,0:T(8,128)(2,1)S(1)}, u32[]{:S(2)}, u32[]{:S(2)}) %collective-permute-start.3) | collective-permute-done | bytes 460832 | tf_op jit(solution)/shard_map/ppermute | solution.py:298
  32.3 0.7 slice.4.refs_0_
  33.0 7.7 %collective-permute-done.4.refs_3_.refs_2_ = bf16[128,1152]{1,0:T(8,128)(2,1)S(1)} collective-permute-done((bf16[128,1152]{1,0:T(8,128)(2,1)}, bf16[128,1152]{1,0:T(8,128)(2,1)S(1)}, u32[]{:S(2)}, u32[]{:S(2)}) %collective-permute-start.4) | collective-permute-done | bytes 294944 | tf_op jit(solution)/shard_map/ppermute | solution.py:298
  40.7 0.7 copy-done.13
  41.4 0.0 all-gather.3.cloned.1.call-update
  41.4 0.0 all-gather.5.cloned.1.call-start
  41.5 1.2 dynamic-slice_select_fusion
  42.7 15.1 %collective-permute-start.11 = (bf16[144,1152]{1,0:T(8,128)(2,1)S(1)}, bf16[144,1152]{1,0:T(8,128)(2,1)S(1)}, u32[]{:S(2)}, u32[]{:S(2)}) collective-permute-start(bf16[144,1152]{1,0:T(8,128)(2,1)S(1)} %dynamic-slice_select_fusion), channel_id=1, source_target_pairs={{0,2},{1,3},{2,0},{3,1},{4,6},{5,7},{6,4},{7,5},{8,10},{9,11},{10,... | collective-permute-start | bytes 995336 | tf_op jit(solution)/shard_map/ppermute | solution.py:298
  57.7 11.8 %shard_map.75 = (bf16[128,1152]{1,0:T(8,128)(2,1)}, bf16[128,1152]{1,0:T(8,128)(2,1)}, bf16[128,1152]{1,0:T(8,128)(2,1)}, bf16[128,1152]{1,0:T(8,128)(2,1)}) custom-call(bf16[128,1152]{1,0:T(8,128)(2,1)} %get-tuple-element.16.refs_0_, bf16[128,1152]{1,0:T(8,128)(2,1)} %copy-done.12, bf16[200,1152]{1,0:T(8,128)(2,1)} %copy-done.14, ...), custom_call_target="tpu_custom_call" | custom-call | flops 4076863488 | bytes 5308416 | tf_op jit(solution)/shard_map/pallas_call | solution.py:120
  69.5 0.1 collective-permute-start.5
  69.6 0.1 collective-permute-start.6
  69.7 5.9 %collective-permute-start.7 = (bf16[128,1152]{1,0:T(8,128)(2,1)}, bf16[128,1152]{1,0:T(8,128)(2,1)S(1)}, u32[]{:S(2)}, u32[]{:S(2)}) collective-permute-start(bf16[128,1152]{1,0:T(8,128)(2,1)} %get-tuple-element.22), channel_id=1, source_target_pairs={{0,3},{1,2},{2,1},{3,0},{4,7},{5,6},{6,5},{7,4},{8,11},{9,10},{10,... | collective-permute-start | bytes 884744 | tf_op jit(solution)/shard_map/ppermute | solution.py:298
  75.7 0.0 collective-permute-done.11.refs_0_
  75.7 0.0 collective-permute-done.5.refs_2_.refs_1_
  75.7 6.4 %collective-permute-done.6.refs_3_.refs_2_ = bf16[128,1152]{1,0:T(8,128)(2,1)S(1)} collective-permute-done((bf16[128,1152]{1,0:T(8,128)(2,1)}, bf16[128,1152]{1,0:T(8,128)(2,1)S(1)}, u32[]{:S(2)}, u32[]{:S(2)}) %collective-permute-start.6) | collective-permute-done | bytes 294944 | tf_op jit(solution)/shard_map/ppermute | solution.py:298
  82.1 7.0 %collective-permute-done.7.refs_4_.refs_3_ = bf16[128,1152]{1,0:T(8,128)(2,1)S(1)} collective-permute-done((bf16[128,1152]{1,0:T(8,128)(2,1)}, bf16[128,1152]{1,0:T(8,128)(2,1)S(1)}, u32[]{:S(2)}, u32[]{:S(2)}) %collective-permute-start.7) | collective-permute-done | bytes 294944 | tf_op jit(solution)/shard_map/ppermute | solution.py:298
  89.1 0.7 copy-done.11
  89.8 0.0 all-gather.5.cloned.1.call-update
  89.8 0.3 collective-permute-start.8
  90.1 0.5 collective-permute-start.9
  90.6 4.3 %shard_map.76 = (f32[4,64,1152]{2,1,0:T(8,128)}, bf16[64,4608]{1,0:T(8,128)(2,1)}) custom-call(s32[1]{0:T(128)} %bitcast.core_ref, f32[4,1152]{1,0:T(4,128)} %embed_ref.1, f32[3,3,1152]{2,1,0:T(4,128)} %mod_ref.7, f32[64,4,1152]{2,1,0:T(4,128)} %refs_0_.2, bf16[128,1152]{1,0:T(8,128)(2,1)} %get-tuple-element.19.refs_1_, bf16[128,1152]{1,0:T(8,128)(2,1)} %copy-done.9, ...), custom_call_target="tpu_custom_call" | custom-call | tf_op jit(solution)/shard_map/pallas_call | solution.py:202
  94.9 1.2 reshape.23
  96.1 42.4 %all_to_all.10 = bf16[64,4,1152]{2,1,0:T(4,128)(2,1)S(1)} all-to-all(bf16[64,4,1152]{2,1,0:T(4,128)(2,1)S(1)} %reshape.23), channel_id=1, replica_groups=mesh['seq'=64,'tp'=4] {'seq'}, dimensions={0} | all-to-all | bytes 1179648 | tf_op jit(solution)/shard_map/all_to_all | solution.py:360
  138.5 0.9 copy.14
  139.4 0.0 collective-permute-done.8.refs_1_.refs_2_
  139.4 0.0 collective-permute-done.9.refs_2_.refs_3_
  139.4 0.0 copy-start.5
  139.4 0.0 all-gather.3.cloned.1.call-done.refs_0_
  139.5 1.8 collective-permute-start.10
  141.3 0.0 copy-done.5
  141.3 7.6 %shard_map.78.refs_1_ = f32[256,1152]{1,0:T(8,128)S(1)} custom-call(bf16[64,4608]{1,0:T(8,128)(2,1)S(1)} %copy-done, bf16[2,864,1152]{2,1,0:T(8,128)(2,1)} %bitcast.16, bf16[2,288,1152]{2,1,0:T(8,128)(2,1)S(1)} %copy-done.5, bf16[2,864,1152]{2,1,0:T(8,128)(2,1)} %collective-permute-done.refs_1_.refs_6_.refs_3_, bf16[2,288,1152]{2,1,0:T(8,128)(2,1)S(1)} %copy-done.4), custom_call_target="tpu_custom_call" | custom-call | flops 2038431744 | bytes 5308416 | tf_op jit(solution)/shard_map/pallas_call | solution.py:120
  148.9 0.0 collective-permute-done.10.refs_3_
  148.9 6.3 %shard_map.81 = bf16[64,4608]{1,0:T(8,128)(2,1)S(1)} custom-call(bf16[64,4608]{1,0:T(8,128)(2,1)S(1)} %copy-done, f32[256,1152]{1,0:T(8,128)S(1)} %shard_map.78.refs_1_, bf16[1152,1152]{1,0:T(8,128)(2,1)S(1)} %copy-done.1, bf16[1152,1152]{1,0:T(8,128)(2,1)S(1)} %collective-permute-done.10.refs_3_), custom_call_target="tpu_custom_call" | custom-call | flops 2038431744 | bytes 5308416 | tf_op jit(solution)/shard_map/pallas_call | solution.py:120
  155.3 0.1 reshape.25
  155.4 24.0 %all_to_all.11 = bf16[64,4,1152]{2,1,0:T(4,128)(2,1)S(1)} all-to-all(bf16[64,4,1152]{2,1,0:T(4,128)(2,1)S(1)} %reshape.25), channel_id=1, replica_groups=mesh['seq'=64,'tp'=4] {'seq'}, dimensions={0} | all-to-all | bytes 1179648 | tf_op jit(solution)/shard_map/all_to_all | solution.py:360
  179.4 0.9 copy.15
  180.3 2.4 %collective-permute-start.12 = (bf16[2304,1152]{1,0:T(8,128)(2,1)}, bf16[2304,1152]{1,0:T(8,128)(2,1)S(1)}, u32[]{:S(2)}, u32[]{:S(2)}) collective-permute-start(bf16[2304,1152]{1,0:T(8,128)(2,1)} %shard_map.83.refs_4_), channel_id=1, source_target_pairs={{0,1},{1,0},{2,3},{3,2},{4,5},{5,4},{6,7},{7,6},{8,9},{9,8},{10,11... | collective-permute-start | bytes 15925256 | tf_op jit(solution)/shard_map/ppermute | solution.py:298
  182.7 9.2 %shard_map.84 = (f32[256,1152]{1,0:T(8,128)S(1)}, bf16[256,1152]{1,0:T(8,128)(2,1)S(1)}) custom-call(f32[3,3,1152]{2,1,0:T(4,128)S(1)} %copy-done.7, f32[4,64,1152]{2,1,0:T(8,128)S(1)} %copy-done.6, bf16[64,4608]{1,0:T(8,128)(2,1)S(1)} %bitcast.12, bf16[1152,1152]{1,0:T(8,128)(2,1)} %refs_0_.3, bf16[1152,1152]{1,0:T(8,128)(2,1)} %refs_1_.1, ...), custom_call_target="tpu_custom_call" | custom-call | flops 4076863488 | bytes 15925248 | tf_op jit(solution)/shard_map/pallas_call | solution.py:276
  191.9 4.3 %shard_map.85 = f32[64,4,1152]{2,1,0:T(4,128)} custom-call(f32[3,3,1152]{2,1,0:T(4,128)S(1)} %copy-done.7, bf16[256,1152]{1,0:T(8,128)(2,1)S(1)} %get-tuple-element.25.in_a, f32[256,1152]{1,0:T(8,128)S(1)} %get-tuple-element.26.in_b, bf16[2304,1152]{1,0:T(8,128)(2,1)S(1)} %collective-permute-done.12.refs_0_), custom_call_target="tpu_custom_call" | custom-call | flops 1358954496 | bytes 5308416 | tf_op jit(solution)/shard_map/pallas_call | solution.py:276
  (36 shorter events, 0.1 us)
Async XLA Ops:
  6.5 132.9 %all-gather.3.cloned.1.call-start = ((), (), s32[]{:S(2)}) async-start(), calls=%async_computation.2 | async-start | bytes 2820096 | tf_op jit(solution)/shard_map/all_gather | solution.py:302
  6.5 13.0 %collective-permute-start = (bf16[2,864,1152]{2,1,0:T(8,128)(2,1)}, bf16[2,864,1152]{2,1,0:T(8,128)(2,1)}, u32[]{:S(2)}, u32[]{:S(2)}) collective-permute-start(bf16[2,864,1152]{2,1,0:T(8,128)(2,1)} %bitcast.13), channel_id=1, source_target_pairs={{0,1},{1,0},{2,3},{3,2},{4,5},{5,4},{6,7},{7,6},{8,9},{9,8},{10,11... | collective-permute-start | bytes 11943944 | tf_op jit(solution)/shard_map/ppermute | solution.py:298
  9.8 9.8 %collective-permute-start.1 = (bf16[2,288,1152]{2,1,0:T(8,128)(2,1)}, bf16[2,288,1152]{2,1,0:T(8,128)(2,1)S(1)}, u32[]{:S(2)}, u32[]{:S(2)}) collective-permute-start(bf16[2,288,1152]{2,1,0:T(8,128)(2,1)} %refs_2_.1), channel_id=1, source_target_pairs={{0,1},{1,0},{2,3},{3,2},{4,5},{5,4},{6,7},{7,6},{8,9},{9,8},{10,11... | collective-permute-start | bytes 3981320 | tf_op jit(solution)/shard_map/ppermute | solution.py:298
  14.4 17.9 %collective-permute-start.3 = (bf16[200,1152]{1,0:T(8,128)(2,1)}, bf16[200,1152]{1,0:T(8,128)(2,1)S(1)}, u32[]{:S(2)}, u32[]{:S(2)}) collective-permute-start(bf16[200,1152]{1,0:T(8,128)(2,1)} %get-tuple-element.18), channel_id=1, source_target_pairs={{0,2},{1,3},{2,0},{3,1},{4,6},{5,7},{6,4},{7,5},{8,10},{9,11},{10,... | collective-permute-start | bytes 1382408 | tf_op jit(solution)/shard_map/ppermute | solution.py:298
  19.6 1.1 copy-start.3
  20.7 12.3 %collective-permute-start.2 = (bf16[128,1152]{1,0:T(8,128)(2,1)}, bf16[128,1152]{1,0:T(8,128)(2,1)S(1)}, u32[]{:S(2)}, u32[]{:S(2)}) collective-permute-start(bf16[128,1152]{1,0:T(8,128)(2,1)} %shard_map.74), channel_id=1, source_target_pairs={{0,1},{1,0},{2,3},{3,2},{4,5},{5,4},{6,7},{7,6},{8,9},{9,8},{10,11... | collective-permute-start | bytes 884744 | tf_op jit(solution)/shard_map/ppermute | solution.py:298
  21.4 19.2 %collective-permute-start.4 = (bf16[128,1152]{1,0:T(8,128)(2,1)}, bf16[128,1152]{1,0:T(8,128)(2,1)S(1)}, u32[]{:S(2)}, u32[]{:S(2)}) collective-permute-start(bf16[128,1152]{1,0:T(8,128)(2,1)} %shard_map.74), channel_id=1, source_target_pairs={{0,3},{1,2},{2,1},{3,0},{4,7},{5,6},{6,5},{7,4},{8,11},{9,10},{10,... | collective-permute-start | bytes 884744 | tf_op jit(solution)/shard_map/ppermute | solution.py:298
  32.3 25.4 %copy-start.14 = (bf16[200,1152]{1,0:T(8,128)(2,1)}, bf16[200,1152]{1,0:T(8,128)(2,1)S(1)}, u32[]{:S(2)}) copy-start(bf16[200,1152]{1,0:T(8,128)(2,1)S(1)} %collective-permute-done.3.refs_2_) | copy-start | bytes 1382404
  33.0 7.7 %copy-start.12 = (bf16[128,1152]{1,0:T(8,128)(2,1)}, bf16[128,1152]{1,0:T(8,128)(2,1)S(1)}, u32[]{:S(2)}) copy-start(bf16[128,1152]{1,0:T(8,128)(2,1)S(1)} %collective-permute-done.2.refs_1_) | copy-start | bytes 884740
  40.7 0.7 copy-start.13
  41.4 138.9 %all-gather.5.cloned.1.call-start = ((), (), s32[]{:S(2)}) async-start(), calls=%async_computation.3 | async-start | bytes 5640192 | tf_op jit(solution)/shard_map/all_gather | solution.py:302
  42.7 33.0 %collective-permute-start.11 = (bf16[144,1152]{1,0:T(8,128)(2,1)S(1)}, bf16[144,1152]{1,0:T(8,128)(2,1)S(1)}, u32[]{:S(2)}, u32[]{:S(2)}) collective-permute-start(bf16[144,1152]{1,0:T(8,128)(2,1)S(1)} %dynamic-slice_select_fusion), channel_id=1, source_target_pairs={{0,2},{1,3},{2,0},{3,1},{4,6},{5,7},{6,4},{7,5},{8,10},{9,11},{10,... | collective-permute-start | bytes 995336 | tf_op jit(solution)/shard_map/ppermute | solution.py:298
  69.5 6.1 %collective-permute-start.5 = (bf16[128,1152]{1,0:T(8,128)(2,1)}, bf16[128,1152]{1,0:T(8,128)(2,1)S(1)}, u32[]{:S(2)}, u32[]{:S(2)}) collective-permute-start(bf16[128,1152]{1,0:T(8,128)(2,1)} %get-tuple-element.20), channel_id=1, source_target_pairs={{0,1},{1,0},{2,3},{3,2},{4,5},{5,4},{6,7},{7,6},{8,9},{9,8},{10,11... | collective-permute-start | bytes 884744 | tf_op jit(solution)/shard_map/ppermute | solution.py:298
  69.6 12.5 %collective-permute-start.6 = (bf16[128,1152]{1,0:T(8,128)(2,1)}, bf16[128,1152]{1,0:T(8,128)(2,1)S(1)}, u32[]{:S(2)}, u32[]{:S(2)}) collective-permute-start(bf16[128,1152]{1,0:T(8,128)(2,1)} %get-tuple-element.21), channel_id=1, source_target_pairs={{0,2},{1,3},{2,0},{3,1},{4,6},{5,7},{6,4},{7,5},{8,10},{9,11},{10,... | collective-permute-start | bytes 884744 | tf_op jit(solution)/shard_map/ppermute | solution.py:298
  69.7 19.3 %collective-permute-start.7 = (bf16[128,1152]{1,0:T(8,128)(2,1)}, bf16[128,1152]{1,0:T(8,128)(2,1)S(1)}, u32[]{:S(2)}, u32[]{:S(2)}) collective-permute-start(bf16[128,1152]{1,0:T(8,128)(2,1)} %get-tuple-element.22), channel_id=1, source_target_pairs={{0,3},{1,2},{2,1},{3,0},{4,7},{5,6},{6,5},{7,4},{8,11},{9,10},{10,... | collective-permute-start | bytes 884744 | tf_op jit(solution)/shard_map/ppermute | solution.py:298
  75.7 13.4 %copy-start.8 = (bf16[144,1152]{1,0:T(8,128)(2,1)}, bf16[144,1152]{1,0:T(8,128)(2,1)S(1)}, u32[]{:S(2)}) copy-start(bf16[144,1152]{1,0:T(8,128)(2,1)S(1)} %collective-permute-done.11.refs_0_) | copy-start | bytes 995332
  75.7 13.4 %copy-start.9 = (bf16[128,1152]{1,0:T(8,128)(2,1)}, bf16[128,1152]{1,0:T(8,128)(2,1)S(1)}, u32[]{:S(2)}) copy-start(bf16[128,1152]{1,0:T(8,128)(2,1)S(1)} %collective-permute-done.5.refs_2_.refs_1_) | copy-start | bytes 884740
  82.1 7.0 %copy-start.10 = (bf16[128,1152]{1,0:T(8,128)(2,1)}, bf16[128,1152]{1,0:T(8,128)(2,1)S(1)}, u32[]{:S(2)}) copy-start(bf16[128,1152]{1,0:T(8,128)(2,1)S(1)} %collective-permute-done.6.refs_3_.refs_2_) | copy-start | bytes 884740
  89.1 0.7 copy-start.11
  89.8 49.6 %collective-permute-start.8 = (bf16[1152,1152]{1,0:T(8,128)(2,1)}, bf16[1152,1152]{1,0:T(8,128)(2,1)}, u32[]{:S(2)}, u32[]{:S(2)}) collective-permute-start(bf16[1152,1152]{1,0:T(8,128)(2,1)} %refs_0_.3), channel_id=1, source_target_pairs={{0,1},{1,0},{2,3},{3,2},{4,5},{5,4},{6,7},{7,6},{8,9},{9,8},{10,11... | collective-permute-start | bytes 7962632 | tf_op jit(solution)/shard_map/ppermute | solution.py:298
  90.1 49.3 %collective-permute-start.9 = (bf16[1152,1152]{1,0:T(8,128)(2,1)}, bf16[1152,1152]{1,0:T(8,128)(2,1)}, u32[]{:S(2)}, u32[]{:S(2)}) collective-permute-start(bf16[1152,1152]{1,0:T(8,128)(2,1)} %refs_1_.1), channel_id=1, source_target_pairs={{0,1},{1,0},{2,3},{3,2},{4,5},{5,4},{6,7},{7,6},{8,9},{9,8},{10,11... | collective-permute-start | bytes 7962632 | tf_op jit(solution)/shard_map/ppermute | solution.py:298
  139.4 1.9 copy-start
  139.4 1.9 copy-start.4
  139.4 1.9 copy-start.5
  139.5 9.5 %copy-start.1 = (bf16[1152,1152]{1,0:T(8,128)(2,1)S(1)}, bf16[1152,1152]{1,0:T(8,128)(2,1)}, u32[]{:S(2)}) copy-start(bf16[1152,1152]{1,0:T(8,128)(2,1)} %shard_map.80.refs_2_) | copy-start | bytes 7962628
  139.5 9.5 %collective-permute-start.10 = (bf16[1152,1152]{1,0:T(8,128)(2,1)}, bf16[1152,1152]{1,0:T(8,128)(2,1)S(1)}, u32[]{:S(2)}, u32[]{:S(2)}) collective-permute-start(bf16[1152,1152]{1,0:T(8,128)(2,1)} %shard_map.80.refs_2_), channel_id=1, source_target_pairs={{0,1},{1,0},{2,3},{3,2},{4,5},{5,4},{6,7},{7,6},{8,9},{9,8},{10,11... | collective-permute-start | bytes 7962632 | tf_op jit(solution)/shard_map/ppermute | solution.py:298
  180.3 2.4 %copy-start.2 = (bf16[8,8,4,1152]{3,1,2,0:T(8,128)(2,1)S(1)}, bf16[8,8,4,1152]{3,1,2,0:T(8,128)(2,1)}, u32[]{:S(2)}) copy-start(bf16[8,8,4,1152]{3,1,2,0:T(8,128)(2,1)} %copy.15) | copy-start | bytes 1769476
  180.3 2.4 %copy-start.6 = (f32[4,64,1152]{2,1,0:T(8,128)S(1)}, f32[4,64,1152]{2,1,0:T(8,128)}, u32[]{:S(2)}) copy-start(f32[4,64,1152]{2,1,0:T(8,128)} %get-tuple-element.23.in_a) | copy-start | bytes 3538948
  180.3 2.4 %copy-start.7 = (f32[3,3,1152]{2,1,0:T(4,128)S(1)}, f32[3,3,1152]{2,1,0:T(4,128)}, u32[]{:S(2)}) copy-start(f32[3,3,1152]{2,1,0:T(4,128)} %mod_ref.7) | copy-start | bytes 124420
  180.3 11.5 %collective-permute-start.12 = (bf16[2304,1152]{1,0:T(8,128)(2,1)}, bf16[2304,1152]{1,0:T(8,128)(2,1)S(1)}, u32[]{:S(2)}, u32[]{:S(2)}) collective-permute-start(bf16[2304,1152]{1,0:T(8,128)(2,1)} %shard_map.83.refs_4_), channel_id=1, source_target_pairs={{0,1},{1,0},{2,3},{3,2},{4,5},{5,4},{6,7},{7,6},{8,9},{9,8},{10,11... | collective-permute-start | bytes 15925256 | tf_op jit(solution)/shard_map/ppermute | solution.py:298
Sparse Core Ops, SparseCore 0:
  41.5 63.9 all-gather.2
  108.0 69.4 all-gather.4
where the time goes:
time: 203 us
  blocking collectives  66.4 us (33%)
  Pallas kernels  46.4 us (23%)
  starting transfers between devices  38.8 us (19%)
  waiting for transfers between devices  28.5 us (14%)
  between operations  13.6 us (7%)
  local copies, waits for them, and re-layouts  6.38 us (3%)
  other arithmetic  2.86 us (1%)
    all_to_all x2, blocking collectives, regroup(): rows = lax.all_to_all(rows, 'seq', split_axis=0, concat_axis=0, tiled=True)  66.4 us
    ppermute x13, starting transfers between devices, swap(): return lax.ppermute(x, 'tp', SWAPS[d])  38.8 us
    ppermute x13, waiting for transfers between devices, swap(): return lax.ppermute(x, 'tp', SWAPS[d])  28.5 us
    pallas_call x3, Pallas kernels, attend(): pl.pallas_call(functools.partial(attend_kernel, pieces, len(inits), layer...  25.7 us
    pallas_call x2, Pallas kernels, mlp(): pl.pallas_call(functools.partial(mlp_kernel, first, len(weights)), out_sh...  13.5 us
    unnamed x32, local copies, waits for them, and re-layouts  4.33 us
    pallas_call x1, Pallas kernels, finish_spatial(): pl.pallas_call(middle_kernel, out_shape=[jax.ShapeDtypeStruct((frames, lo...  4.29 us
  transfers between devices with their start and end apart: 15, of which 4 were waited for; matrix products, arithmetic and copies ran while one was open for 3% of the time, Pallas kernels for 21%

commit v1 on v0

--- a/solution.py
+++ b/solution.py
@@ -22,8 +22,9 @@
 def attend_kernel(pieces, ready, layer, *refs):
     x_refs, refs = refs[:pieces], refs[pieces:]
     inits, refs = refs[:ready], refs[ready:]
-    out_refs, (held, sems, stage, out_sems, came) = refs[-pieces - 5 : -5], refs[-5:]
-    sources = refs[: -pieces - 5]
+    results = 2 if pieces == 1 and not ready else pieces
+    out_refs, (held, sems, stage, out_sems, came, rows4) = refs[-results - 6 : -6], refs[-6:]
+    sources = refs[: -results - 6]
     heads = 4
     width = heads * HD
     length = 256
@@ -49,10 +50,13 @@
     for copy in copies[:each]:
         copy.start()
     model = held.shape[2]
-    if wide:
-        part = x_refs[0].shape[0]
-        spans = [slice(j * model, (j + 1) * model) for j in range(length // part)]
-        x = jnp.concatenate([x_refs[0][:, span] for span in spans], axis=0)
+    if ready:
+        x = x_refs[0][...]
+    elif wide:
+        frames = x_refs[0].shape[1]
+        rows4[...] = x_refs[0][...].astype(F32)
+        x = jnp.concatenate([rows4[:, j, :].astype(BF) for j in range(frames)], axis=0)
+        out_refs[1][...] = x
     else:
         for arrival in arrivals:
             arrival.wait()
@@ -88,8 +92,8 @@
     total = shard(0) + shard(1)
     if ready:
         total = total + inits[0][...]
-    total = total.astype(out_refs[0].dtype)
     if not wide:
+        total = total.astype(BF)
         sends = []
         for d in reversed(range(pieces)):
             for s in range(items):
@@ -100,8 +104,10 @@
         for send in sends:
             send.wait()
     elif ready:
-        for j, span in enumerate(spans):
-            out_refs[0][:, span] = total[j * part : (j + 1) * part]
+        total = total.astype(BF)
+        part = out_refs[0].shape[0]
+        for j in range(length // part):
+            out_refs[0][:, j * model : (j + 1) * model] = total[j * part : (j + 1) * part]
     else:
         out_refs[0][...] = total
 
@@ -115,21 +121,24 @@
     rows = parts[0].size * pieces // width
     limit = 62 if pieces > 1 else 24 if inits else 48
     outs = [jax.ShapeDtypeStruct(parts[0].shape, BF)] * pieces
-    if pieces == 1 and not inits:
-        outs = [jax.ShapeDtypeStruct((rows, width), F32)]
+    if pieces == 1:
+        outs = [jax.ShapeDtypeStruct((rows, width), kind) for kind in (F32, BF)]
+    if inits:
+        outs = [jax.ShapeDtypeStruct((rows // 4, 4 * width), BF)]
     return pl.pallas_call(
         functools.partial(attend_kernel, pieces, len(inits), layer),
         out_shape=outs,
         in_specs=[vmem if pieces == 1 else free] * pieces
         + [vmem] * len(inits)
         + [free] * len(weights),
-        out_specs=[vmem if pieces == 1 else hbm] * pieces,
+        out_specs=[vmem if pieces == 1 else hbm] * len(outs),
         scratch_shapes=[
             pltpu.VMEM((2, width, width), BF),
             pltpu.SemaphoreType.DMA((len(weights),)),
             pltpu.VMEM((pieces, *parts[0].shape) if pieces > 1 else (1, 16, 128), BF),
             pltpu.SemaphoreType.DMA((pieces,)),
             pltpu.VMEM((pieces, *parts[0].shape) if pieces > 1 else (1, 16, 128), BF),
+            pltpu.VMEM(parts[0].shape if len(outs) == 2 else (8, 4, 128), F32),
         ],
         compiler_params=pltpu.CompilerParams(vmem_limit_bytes=limit * 2**20),
         cost_estimate=pl.CostEstimate(
@@ -175,7 +184,7 @@
 
 
 def middle_kernel(core_ref, embed_ref, mod_ref, *refs):
-    sources, (mid_ref, norm_ref), held, sems = refs[:5], refs[5:7], refs[7:12], refs[12]
+    sources, (mid_ref, norm_ref), held, sems, wide = refs[:5], refs[5:7], refs[7:12], refs[12], refs[13]
     copies = [
         pltpu.make_async_copy(a, b, sems.at[i]) for i, (a, b) in enumerate(zip(sources, held))
     ]
@@ -184,7 +193,7 @@
     for copy in copies:
         copy.wait()
     lat_ref, b0, b1, b2, b3 = held
-    part, _, model = lat_ref.shape
+    part = lat_ref.shape[0]
     low = core_ref[0] == 0
     for f in range(4):
         span = slice((f % 2) * part, (f % 2 + 1) * part)
@@ -193,7 +202,8 @@
         added = jnp.where(low, mine, theirs) if f < 2 else jnp.where(low, theirs, mine)
         x = lat_ref[:, f, :] + mod_ref[0, 2:3, :] * added + embed_ref[f : f + 1, :]
         mid_ref[f] = x
-        norm_ref[:, f * model : (f + 1) * model] = norm_rows(x, mod_ref, 1)
+        wide[:, f, :] = norm_rows(x, mod_ref, 1).astype(F32)
+    norm_ref[...] = wide[...].astype(BF)
 
 
 def finish_spatial(core, latents, time_embed, modulation, back):
@@ -203,7 +213,7 @@
         middle_kernel,
         out_shape=[
             jax.ShapeDtypeStruct((frames, local, width), F32),
-            jax.ShapeDtypeStruct((local, frames * width), BF),
+            jax.ShapeDtypeStruct((local, frames, width), BF),
         ],
         in_specs=[pl.BlockSpec(memory_space=pltpu.SMEM)]
         + [vmem] * 2
@@ -211,14 +221,14 @@
         out_specs=[vmem] * 2,
         scratch_shapes=[pltpu.VMEM(latents.shape, F32)]
         + [pltpu.VMEM(part.shape, BF) for part in back]
-        + [pltpu.SemaphoreType.DMA((5,))],
+        + [pltpu.SemaphoreType.DMA((5,)), pltpu.VMEM(latents.shape, F32)],
         compiler_params=pltpu.CompilerParams(vmem_limit_bytes=62 * 2**20),
     )(core.reshape(1), time_embed, modulation, latents, *back)
 
 
 def mlp_kernel(first, count, mod_ref, in_a, in_b, *refs):
     sources, refs = refs[:count], refs[count:]
-    outs, (held, sems, held_a, held_b, in_sems) = refs[:-5], refs[-5:]
+    outs, (held, sems, held_a, held_b, in_sems, rows4) = refs[:-6], refs[-6:]
     width = held.shape[2]
     blocks = []
     for ref in sources:
@@ -236,9 +246,9 @@
         arrivals[1].wait()
         base_ref, x_ref = outs
         local = held_b.shape[0]
+        rows4[...] = held_b[...].astype(F32)
         for f in range(held_a.shape[0]):
-            arrived = held_b[:, f * width : (f + 1) * width].astype(F32)
-            hidden = held_a[f] + mod_ref[1, 2:3, :] * arrived
+            hidden = held_a[f] + mod_ref[1, 2:3, :] * rows4[:, f, :]
             base_ref[f * local : (f + 1) * local] = hidden
             x_ref[f * local : (f + 1) * local] = norm_rows(hidden, mod_ref, 2)
     else:
@@ -284,6 +294,7 @@
             pltpu.VMEM(inputs[0].shape, inputs[0].dtype),
             pltpu.VMEM(inputs[1].shape, inputs[1].dtype),
             pltpu.SemaphoreType.DMA((2,)),
+            pltpu.VMEM(inputs[1].shape if first else (8, 4, 128), F32),
         ],
         compiler_params=pltpu.CompilerParams(vmem_limit_bytes=limit * 2**20),
         cost_estimate=pl.CostEstimate(
@@ -336,35 +347,34 @@
         lax.dynamic_slice(qkv, (1, place * cut, 0), (1, cut, width))[0],
         lax.dynamic_slice(out_weight, (1, (place - 12) * cut, 0), (1, cut, width))[0],
     )
-    keep, give, send = enter_spatial(core, latents, modulation, piece_t)
-    give = after(give, other_qkv, other_out)
-    parts = [keep, swap(give, 1), swap(send, 2), swap(give, 3)]
-    far_t = gather(after(parts[2][2 * latents.shape[0] :], parts[1], parts[3]))
-
     cut = width // 8
     piece_f = jnp.where(
         place < 8,
         lax.dynamic_slice_in_dim(mlp_in_weight, place * cut, cut, axis=0),
         lax.dynamic_slice_in_dim(mlp_out_weight, (place - 8) * cut, cut, axis=0),
     )
+    keep, give, send = enter_spatial(core, latents, modulation, piece_t)
+    give = after(give, other_qkv, other_out, piece_f)
+    parts = [keep, swap(give, 1), swap(send, 2), swap(give, 3)]
+    far_t = gather(after(parts[2][2 * latents.shape[0] :], parts[1], parts[3]))
+
     moved = swap(piece_f, 2)
     back = attend(0, parts, near)
+    far_f = gather(after(moved, back[0]))
     back = [(back[0] if d == 0 else swap(back[d], d)) for d in range(4)]
-    far_f = gather(after(moved, *back[1:]))
     middle, normed = finish_spatial(core, latents, time_embed, modulation, back)
     other_mlp_in = swap(mlp_in_weight, 1)
     other_mlp_out = swap(mlp_out_weight, 1)
 
     def regroup(rows):
         rows = rows.reshape(latents.shape)
-        rows = lax.all_to_all(rows, "seq", split_axis=0, concat_axis=0, tiled=True)
-        return rows.reshape(rows.shape[0], -1)
-
-    regrouped = after(regroup(normed), other_mlp_in, other_mlp_out)
-    partial = attend(1, [regrouped], near)
-    far_t = after(far_t, regrouped)
+        return lax.all_to_all(rows, "seq", split_axis=0, concat_axis=0, tiled=True)
+
+    regrouped = regroup(normed)
+    partial, rows = attend(1, [regrouped], near)
+    far_t = after(far_t, middle, other_mlp_in, other_mlp_out)
     far_other_t = swap(far_t, 1)
-    (projected,) = attend(1, [regrouped], (far_t, far_other_t), partial)
+    (projected,) = attend(1, [rows], (far_t, far_other_t), [partial])
     projected = regroup(projected)
     far_f = after(far_f, projected)
     far_other_f = swap(far_f, 1)

time: 203 us -> 200 us (0.985)
  waiting for transfers between devices: 28.5 us -> 40.7 us
  blocking collectives: 66.4 us -> 56 us
  starting transfers between devices: 38.8 us -> 34.5 us
  local copies, waits for them, and re-layouts: 6.38 us -> 4.24 us
    all_gather x2, waiting for transfers between devices: 0.02 us -> 12.2 us  [gather(): lax.all_gather(piece, 'seq', axis=0, tiled=True, axis_index_groups=PLANE)]
    all_to_all x2, blocking collectives: 66.4 us -> 56 us  [regroup(): return lax.all_to_all(rows, 'seq', split_axis=0, concat_axis=0, tiled=True)]
    ppermute x13, starting transfers between devices: 38.8 us -> 34.4 us  [swap(): return lax.ppermute(x, 'tp', SWAPS[d])]
  transfers between devices with their start and end apart: 15 -> 15, of which waited for: 4 -> 6; matrix products, arithmetic and copies ran while one was open for 3% -> 2% of each run, Pallas kernels for 21% -> 22%
where the time goes in v1:
time: 200 us
  blocking collectives  56 us (28%)
  Pallas kernels  47.4 us (24%)
  waiting for transfers between devices  40.7 us (20%)
  starting transfers between devices  34.5 us (17%)
  between operations  13.6 us (7%)
  local copies, waits for them, and re-layouts  4.24 us (2%)
  other arithmetic  3.57 us (2%)
    all_to_all x2, blocking collectives, regroup(): return lax.all_to_all(rows, 'seq', split_axis=0, concat_axis=0, tiled=True)  56 us
    ppermute x13, starting transfers between devices, swap(): return lax.ppermute(x, 'tp', SWAPS[d])  34.4 us
    ppermute x13, waiting for transfers between devices, swap(): return lax.ppermute(x, 'tp', SWAPS[d])  28.4 us
    pallas_call x3, Pallas kernels, attend(): pl.pallas_call(functools.partial(attend_kernel, pieces, len(inits), layer...  26 us
    pallas_call x2, Pallas kernels, mlp(): pl.pallas_call(functools.partial(mlp_kernel, first, len(weights)), out_sh...  13.5 us
    all_gather x2, waiting for transfers between devices, gather(): lax.all_gather(piece, 'seq', axis=0, tiled=True, axis_index_groups=PLANE)  12.2 us
    pallas_call x1, Pallas kernels, finish_spatial(): pl.pallas_call(middle_kernel, out_shape=[jax.ShapeDtypeStruct((frames, lo...  4.95 us
  transfers between devices with their start and end apart: 15, of which 6 were waited for; matrix products, arithmetic and copies ran while one was open for 2% of the time, Pallas kernels for 22%

profile of v1, /device:TPU:1, one launch (start us, length us, event | category | flops | bytes accessed | tf_op | source)
XLA Modules:
  0.0 199.9 jit_solution(4400287538159191035)
XLA Ops:
  6.5 3.2 %collective-permute-start = (bf16[2,864,1152]{2,1,0:T(8,128)(2,1)}, bf16[2,864,1152]{2,1,0:T(8,128)(2,1)}, u32[]{:S(2)}, u32[]{:S(2)}) collective-permute-start(bf16[2,864,1152]{2,1,0:T(8,128)(2,1)} %bitcast.6), channel_id=1, source_target_pairs={{0,1},{1,0},{2,3},{3,2},{4,5},{5,4},{6,7},{7,6},{8,9},{9,8},{10,11... | collective-permute-start | bytes 11943944 | tf_op jit(solution)/shard_map/ppermute | solution.py:309
  9.8 0.0 collective-permute-start.1
  9.8 1.7 select_bitcast_fusion.piece_ref
  11.5 2.9 %shard_map.73 = (bf16[128,1152]{1,0:T(8,128)(2,1)}, bf16[128,1152]{1,0:T(8,128)(2,1)}, bf16[200,1152]{1,0:T(8,128)(2,1)}) custom-call(s32[1]{0:T(128)} %bitcast.core_ref, f32[64,4,1152]{2,1,0:T(4,128)} %refs_0_.2, f32[3,3,1152]{2,1,0:T(4,128)} %mod_ref.7, bf16[72,1152]{1,0:T(8,128)(2,1)} %select_bitcast_fusion.piece_ref), custom_call_target="tpu_custom_call" | custom-call | tf_op jit(solution)/shard_map/pallas_call | solution.py:177
  14.4 5.2 %collective-permute-start.3 = (bf16[200,1152]{1,0:T(8,128)(2,1)}, bf16[200,1152]{1,0:T(8,128)(2,1)S(1)}, u32[]{:S(2)}, u32[]{:S(2)}) collective-permute-start(bf16[200,1152]{1,0:T(8,128)(2,1)} %get-tuple-element.20), channel_id=1, source_target_pairs={{0,2},{1,3},{2,0},{3,1},{4,6},{5,7},{6,4},{7,5},{8,10},{9,11},{10,... | collective-permute-start | bytes 1382408 | tf_op jit(solution)/shard_map/ppermute | solution.py:309
  19.6 1.9 dynamic-slice_select_fusion.refs_3_
  21.4 0.0 collective-permute-done.1.refs_2_.refs_7_.refs_4_
  21.4 0.0 collective-permute-done.refs_1_.refs_6_.refs_3_
  21.4 1.1 copy-done.2
  22.5 0.8 collective-permute-start.2
  23.3 1.6 collective-permute-start.4
  24.9 7.4 %collective-permute-done.3.refs_2_ = bf16[200,1152]{1,0:T(8,128)(2,1)S(1)} collective-permute-done((bf16[200,1152]{1,0:T(8,128)(2,1)}, bf16[200,1152]{1,0:T(8,128)(2,1)S(1)}, u32[]{:S(2)}, u32[]{:S(2)}) %collective-permute-start.3) | collective-permute-done | bytes 460832 | tf_op jit(solution)/shard_map/ppermute | solution.py:309
  32.3 0.7 slice.4.refs_0_
  33.0 7.7 %collective-permute-done.4.refs_3_.refs_2_ = bf16[128,1152]{1,0:T(8,128)(2,1)S(1)} collective-permute-done((bf16[128,1152]{1,0:T(8,128)(2,1)}, bf16[128,1152]{1,0:T(8,128)(2,1)S(1)}, u32[]{:S(2)}, u32[]{:S(2)}) %collective-permute-start.4) | collective-permute-done | bytes 294944 | tf_op jit(solution)/shard_map/ppermute | solution.py:309
  40.7 0.7 copy-done.11
  41.4 0.0 all-gather.3.cloned.1.call-update
  41.4 0.0 all-gather.5.cloned.1.call-start
  41.5 13.9 %collective-permute-start.11 = (bf16[144,1152]{1,0:T(8,128)(2,1)S(1)}, bf16[144,1152]{1,0:T(8,128)(2,1)S(1)}, u32[]{:S(2)}, u32[]{:S(2)}) collective-permute-start(bf16[144,1152]{1,0:T(8,128)(2,1)S(1)} %copy-done.8), channel_id=1, source_target_pairs={{0,2},{1,3},{2,0},{3,1},{4,6},{5,7},{6,4},{7,5},{8,10},{9,11},{10,... | collective-permute-start | bytes 995336 | tf_op jit(solution)/shard_map/ppermute | solution.py:309
  55.4 11.8 %shard_map.75 = (bf16[128,1152]{1,0:T(8,128)(2,1)}, bf16[128,1152]{1,0:T(8,128)(2,1)}, bf16[128,1152]{1,0:T(8,128)(2,1)}, bf16[128,1152]{1,0:T(8,128)(2,1)}) custom-call(bf16[128,1152]{1,0:T(8,128)(2,1)} %get-tuple-element.18.refs_0_, bf16[128,1152]{1,0:T(8,128)(2,1)} %copy-done.10, bf16[200,1152]{1,0:T(8,128)(2,1)} %copy-done.15, ...), custom_call_target="tpu_custom_call" | custom-call | flops 4076863488 | bytes 5308416 | tf_op jit(solution)/shard_map/pallas_call | solution.py:128
  67.2 0.0 collective-permute-done.11.refs_0_
  67.2 0.7 copy-done.7
  68.0 0.0 all-gather.5.cloned.1.call-update
  68.0 0.1 collective-permute-start.8
  68.1 0.5 collective-permute-start.9
  68.6 0.1 collective-permute-start.5
  68.7 0.0 collective-permute-start.6
  68.7 5.9 %collective-permute-start.7 = (bf16[128,1152]{1,0:T(8,128)(2,1)}, bf16[128,1152]{1,0:T(8,128)(2,1)S(1)}, u32[]{:S(2)}, u32[]{:S(2)}) collective-permute-start(bf16[128,1152]{1,0:T(8,128)(2,1)} %get-tuple-element.24), channel_id=1, source_target_pairs={{0,3},{1,2},{2,1},{3,0},{4,7},{5,6},{6,5},{7,4},{8,11},{9,10},{10,... | collective-permute-start | bytes 884744 | tf_op jit(solution)/shard_map/ppermute | solution.py:309
  74.6 0.0 collective-permute-done.5.refs_2_
  74.6 6.3 %collective-permute-done.6.refs_3_ = bf16[128,1152]{1,0:T(8,128)(2,1)S(1)} collective-permute-done((bf16[128,1152]{1,0:T(8,128)(2,1)}, bf16[128,1152]{1,0:T(8,128)(2,1)S(1)}, u32[]{:S(2)}, u32[]{:S(2)}) %collective-permute-start.6) | collective-permute-done | bytes 294944 | tf_op jit(solution)/shard_map/ppermute | solution.py:309
  81.0 7.0 %collective-permute-done.7.refs_4_ = bf16[128,1152]{1,0:T(8,128)(2,1)S(1)} collective-permute-done((bf16[128,1152]{1,0:T(8,128)(2,1)}, bf16[128,1152]{1,0:T(8,128)(2,1)S(1)}, u32[]{:S(2)}, u32[]{:S(2)}) %collective-permute-start.7) | collective-permute-done | bytes 294944 | tf_op jit(solution)/shard_map/ppermute | solution.py:309
  88.0 0.7 copy-done.14
  88.7 5.0 %shard_map.76 = (f32[4,64,1152]{2,1,0:T(8,128)}, bf16[64,4,1152]{2,1,0:T(4,128)(2,1)}) custom-call(s32[1]{0:T(128)} %bitcast.core_ref, f32[4,1152]{1,0:T(4,128)} %embed_ref.1, f32[3,3,1152]{2,1,0:T(4,128)} %mod_ref.7, f32[64,4,1152]{2,1,0:T(4,128)} %refs_0_.2, bf16[128,1152]{1,0:T(8,128)(2,1)} %get-tuple-element.21.refs_1_, bf16[128,1152]{1,0:T(8,128)(2,1)} %copy-done.12, ...), custom_call_target="tpu_custom_call" | custom-call | tf_op jit(solution)/shard_map/pallas_call | solution.py:212
  93.7 0.0 collective-permute-done.8.refs_2_
  93.7 0.0 collective-permute-done.9.refs_3_
  93.7 11.9 %all-gather.3.cloned.1.call-done.refs_0_ = bf16[1152,1152]{1,0:T(8,128)(2,1)} async-done(((bf16[72,1152]{1,0:T(8,128)(2,1)}), bf16[1152,1152]{1,0:T(8,128)(2,1)}) %all-gather.3.cloned.1.call-update) | async-done | bytes 2654224 | tf_op jit(solution)/shard_map/all_gather | solution.py:313
  105.6 1.0 collective-permute-start.10
  106.6 0.1 copy-done.9
  106.7 32.1 %all_to_all.10.refs_0_ = bf16[64,4,1152]{2,1,0:T(4,128)(2,1)S(1)} all-to-all(bf16[64,4,1152]{2,1,0:T(4,128)(2,1)S(1)} %copy-done.9), channel_id=1, replica_groups=mesh['seq'=64,'tp'=4] {'seq'}, dimensions={0} | all-to-all | bytes 1179648 | tf_op jit(solution)/shard_map/all_to_all | solution.py:371
  138.8 7.9 %shard_map.77 = (f32[256,1152]{1,0:T(8,128)S(1)}, bf16[256,1152]{1,0:T(8,128)(2,1)S(1)}) custom-call(bf16[64,4,1152]{2,1,0:T(4,128)(2,1)S(1)} %all_to_all.10.refs_0_, bf16[2,864,1152]{2,1,0:T(8,128)(2,1)} %bitcast.9, bf16[2,288,1152]{2,1,0:T(8,128)(2,1)S(1)} %copy-done.5, bf16[2,864,1152]{2,1,0:T(8,128)(2,1)} %collective-permute-done.refs_1_.refs_6_.refs_3_, ...), custom_call_target="tpu_custom_call" | custom-call | flops 2038431744 | bytes 5308416 | tf_op jit(solution)/shard_map/pallas_call | solution.py:128
  146.7 0.0 collective-permute-done.10.refs_3_
  146.7 6.3 %shard_map.80 = bf16[64,4608]{1,0:T(8,128)(2,1)S(1)} custom-call(bf16[256,1152]{1,0:T(8,128)(2,1)S(1)} %get-tuple-element.27.refs_0_, f32[256,1152]{1,0:T(8,128)S(1)} %get-tuple-element.28.refs_1_, bf16[1152,1152]{1,0:T(8,128)(2,1)S(1)} %copy-done, bf16[1152,1152]{1,0:T(8,128)(2,1)S(1)} %collective-permute-done.10.refs_3_), custom_call_target="tpu_custom_call" | custom-call | flops 2038431744 | bytes 5308416 | tf_op jit(solution)/shard_map/pallas_call | solution.py:128
  153.0 0.1 reshape.14
  153.2 23.9 %all_to_all.11.refs_1_.in_b = bf16[64,4,1152]{2,1,0:T(4,128)(2,1)} all-to-all(bf16[64,4,1152]{2,1,0:T(4,128)(2,1)S(1)} %reshape.14), channel_id=1, replica_groups=mesh['seq'=64,'tp'=4] {'seq'}, dimensions={0} | all-to-all | bytes 1179648 | tf_op jit(solution)/shard_map/all_to_all | solution.py:371
  177.1 0.3 all-gather.5.cloned.1.call-done.refs_0_
  177.4 2.1 %collective-permute-start.12 = (bf16[2304,1152]{1,0:T(8,128)(2,1)}, bf16[2304,1152]{1,0:T(8,128)(2,1)S(1)}, u32[]{:S(2)}, u32[]{:S(2)}) collective-permute-start(bf16[2304,1152]{1,0:T(8,128)(2,1)} %shard_map.82.refs_4_), channel_id=1, source_target_pairs={{0,1},{1,0},{2,3},{3,2},{4,5},{5,4},{6,7},{7,6},{8,9},{9,8},{10,11... | collective-permute-start | bytes 15925256 | tf_op jit(solution)/shard_map/ppermute | solution.py:309
  179.5 9.2 %shard_map.83 = (f32[256,1152]{1,0:T(8,128)S(1)}, bf16[256,1152]{1,0:T(8,128)(2,1)S(1)}) custom-call(f32[3,3,1152]{2,1,0:T(4,128)S(1)} %copy-done.6, f32[4,64,1152]{2,1,0:T(8,128)S(1)} %copy-done.4, bf16[64,4,1152]{2,1,0:T(4,128)(2,1)S(1)} %copy-done.1, bf16[1152,1152]{1,0:T(8,128)(2,1)} %refs_0_.3, bf16[1152,1152]{1,0:T(8,128)(2,1)} %refs_1_.1, ...), custom_call_target="tpu_custom_call" | custom-call | flops 4076863488 | bytes 15925248 | tf_op jit(solution)/shard_map/pallas_call | solution.py:286
  188.7 0.0 collective-permute-done.12.refs_0_
  188.7 4.3 %shard_map.84 = f32[64,4,1152]{2,1,0:T(4,128)} custom-call(f32[3,3,1152]{2,1,0:T(4,128)S(1)} %copy-done.6, bf16[256,1152]{1,0:T(8,128)(2,1)S(1)} %get-tuple-element.29.in_a, f32[256,1152]{1,0:T(8,128)S(1)} %get-tuple-element.30.in_b, bf16[2304,1152]{1,0:T(8,128)(2,1)S(1)} %collective-permute-done.12.refs_0_), custom_call_target="tpu_custom_call" | custom-call | flops 1358954496 | bytes 5308416 | tf_op jit(solution)/shard_map/pallas_call | solution.py:286
  (34 shorter events, 0.1 us)
Async XLA Ops:
  6.5 99.1 %all-gather.3.cloned.1.call-start = ((), (), s32[]{:S(2)}) async-start(), calls=%async_computation.2 | async-start | bytes 2820096 | tf_op jit(solution)/shard_map/all_gather | solution.py:313
  6.5 14.9 %collective-permute-start = (bf16[2,864,1152]{2,1,0:T(8,128)(2,1)}, bf16[2,864,1152]{2,1,0:T(8,128)(2,1)}, u32[]{:S(2)}, u32[]{:S(2)}) collective-permute-start(bf16[2,864,1152]{2,1,0:T(8,128)(2,1)} %bitcast.6), channel_id=1, source_target_pairs={{0,1},{1,0},{2,3},{3,2},{4,5},{5,4},{6,7},{7,6},{8,9},{9,8},{10,11... | collective-permute-start | bytes 11943944 | tf_op jit(solution)/shard_map/ppermute | solution.py:309
  9.8 11.7 %collective-permute-start.1 = (bf16[2,288,1152]{2,1,0:T(8,128)(2,1)}, bf16[2,288,1152]{2,1,0:T(8,128)(2,1)S(1)}, u32[]{:S(2)}, u32[]{:S(2)}) collective-permute-start(bf16[2,288,1152]{2,1,0:T(8,128)(2,1)} %refs_2_.1), channel_id=1, source_target_pairs={{0,1},{1,0},{2,3},{3,2},{4,5},{5,4},{6,7},{7,6},{8,9},{9,8},{10,11... | collective-permute-start | bytes 3981320 | tf_op jit(solution)/shard_map/ppermute | solution.py:309
  14.4 17.9 %collective-permute-start.3 = (bf16[200,1152]{1,0:T(8,128)(2,1)}, bf16[200,1152]{1,0:T(8,128)(2,1)S(1)}, u32[]{:S(2)}, u32[]{:S(2)}) collective-permute-start(bf16[200,1152]{1,0:T(8,128)(2,1)} %get-tuple-element.20), channel_id=1, source_target_pairs={{0,2},{1,3},{2,0},{3,1},{4,6},{5,7},{6,4},{7,5},{8,10},{9,11},{10,... | collective-permute-start | bytes 1382408 | tf_op jit(solution)/shard_map/ppermute | solution.py:309
  21.4 1.1 copy-start.2
  22.5 19.0 %copy-start.8 = (bf16[144,1152]{1,0:T(8,128)(2,1)S(1)}, bf16[144,1152]{1,0:T(8,128)(2,1)}, u32[]{:S(2)}) copy-start(bf16[144,1152]{1,0:T(8,128)(2,1)} %dynamic-slice_select_fusion.refs_3_) | copy-start | bytes 995332
  22.5 10.5 %collective-permute-start.2 = (bf16[128,1152]{1,0:T(8,128)(2,1)}, bf16[128,1152]{1,0:T(8,128)(2,1)S(1)}, u32[]{:S(2)}, u32[]{:S(2)}) collective-permute-start(bf16[128,1152]{1,0:T(8,128)(2,1)} %shard_map.74), channel_id=1, source_target_pairs={{0,1},{1,0},{2,3},{3,2},{4,5},{5,4},{6,7},{7,6},{8,9},{9,8},{10,11... | collective-permute-start | bytes 884744 | tf_op jit(solution)/shard_map/ppermute | solution.py:309
  23.3 17.3 %collective-permute-start.4 = (bf16[128,1152]{1,0:T(8,128)(2,1)}, bf16[128,1152]{1,0:T(8,128)(2,1)S(1)}, u32[]{:S(2)}, u32[]{:S(2)}) collective-permute-start(bf16[128,1152]{1,0:T(8,128)(2,1)} %shard_map.74), channel_id=1, source_target_pairs={{0,3},{1,2},{2,1},{3,0},{4,7},{5,6},{6,5},{7,4},{8,11},{9,10},{10,... | collective-permute-start | bytes 884744 | tf_op jit(solution)/shard_map/ppermute | solution.py:309
  32.3 23.1 %copy-start.15 = (bf16[200,1152]{1,0:T(8,128)(2,1)}, bf16[200,1152]{1,0:T(8,128)(2,1)S(1)}, u32[]{:S(2)}) copy-start(bf16[200,1152]{1,0:T(8,128)(2,1)S(1)} %collective-permute-done.3.refs_2_) | copy-start | bytes 1382404
  33.0 7.7 %copy-start.10 = (bf16[128,1152]{1,0:T(8,128)(2,1)}, bf16[128,1152]{1,0:T(8,128)(2,1)S(1)}, u32[]{:S(2)}) copy-start(bf16[128,1152]{1,0:T(8,128)(2,1)S(1)} %collective-permute-done.2.refs_1_) | copy-start | bytes 884740
  40.7 0.7 copy-start.11
  41.4 135.9 %all-gather.5.cloned.1.call-start = ((), (), s32[]{:S(2)}) async-start(), calls=%async_computation.3 | async-start | bytes 5640192 | tf_op jit(solution)/shard_map/all_gather | solution.py:313
  41.5 25.7 %collective-permute-start.11 = (bf16[144,1152]{1,0:T(8,128)(2,1)S(1)}, bf16[144,1152]{1,0:T(8,128)(2,1)S(1)}, u32[]{:S(2)}, u32[]{:S(2)}) collective-permute-start(bf16[144,1152]{1,0:T(8,128)(2,1)S(1)} %copy-done.8), channel_id=1, source_target_pairs={{0,2},{1,3},{2,0},{3,1},{4,6},{5,7},{6,4},{7,5},{8,10},{9,11},{10,... | collective-permute-start | bytes 995336 | tf_op jit(solution)/shard_map/ppermute | solution.py:309
  67.2 0.7 copy-start.7
  68.0 25.7 %collective-permute-start.8 = (bf16[1152,1152]{1,0:T(8,128)(2,1)}, bf16[1152,1152]{1,0:T(8,128)(2,1)}, u32[]{:S(2)}, u32[]{:S(2)}) collective-permute-start(bf16[1152,1152]{1,0:T(8,128)(2,1)} %refs_0_.3), channel_id=1, source_target_pairs={{0,1},{1,0},{2,3},{3,2},{4,5},{5,4},{6,7},{7,6},{8,9},{9,8},{10,11... | collective-permute-start | bytes 7962632 | tf_op jit(solution)/shard_map/ppermute | solution.py:309
  68.1 25.6 %collective-permute-start.9 = (bf16[1152,1152]{1,0:T(8,128)(2,1)}, bf16[1152,1152]{1,0:T(8,128)(2,1)}, u32[]{:S(2)}, u32[]{:S(2)}) collective-permute-start(bf16[1152,1152]{1,0:T(8,128)(2,1)} %refs_1_.1), channel_id=1, source_target_pairs={{0,1},{1,0},{2,3},{3,2},{4,5},{5,4},{6,7},{7,6},{8,9},{9,8},{10,11... | collective-permute-start | bytes 7962632 | tf_op jit(solution)/shard_map/ppermute | solution.py:309
  68.6 6.1 %collective-permute-start.5 = (bf16[128,1152]{1,0:T(8,128)(2,1)}, bf16[128,1152]{1,0:T(8,128)(2,1)S(1)}, u32[]{:S(2)}, u32[]{:S(2)}) collective-permute-start(bf16[128,1152]{1,0:T(8,128)(2,1)} %get-tuple-element.22), channel_id=1, source_target_pairs={{0,1},{1,0},{2,3},{3,2},{4,5},{5,4},{6,7},{7,6},{8,9},{9,8},{10,11... | collective-permute-start | bytes 884744 | tf_op jit(solution)/shard_map/ppermute | solution.py:309
  68.7 12.3 %collective-permute-start.6 = (bf16[128,1152]{1,0:T(8,128)(2,1)}, bf16[128,1152]{1,0:T(8,128)(2,1)S(1)}, u32[]{:S(2)}, u32[]{:S(2)}) collective-permute-start(bf16[128,1152]{1,0:T(8,128)(2,1)} %get-tuple-element.23), channel_id=1, source_target_pairs={{0,2},{1,3},{2,0},{3,1},{4,6},{5,7},{6,4},{7,5},{8,10},{9,11},{10,... | collective-permute-start | bytes 884744 | tf_op jit(solution)/shard_map/ppermute | solution.py:309
  68.7 19.3 %collective-permute-start.7 = (bf16[128,1152]{1,0:T(8,128)(2,1)}, bf16[128,1152]{1,0:T(8,128)(2,1)S(1)}, u32[]{:S(2)}, u32[]{:S(2)}) collective-permute-start(bf16[128,1152]{1,0:T(8,128)(2,1)} %get-tuple-element.24), channel_id=1, source_target_pairs={{0,3},{1,2},{2,1},{3,0},{4,7},{5,6},{6,5},{7,4},{8,11},{9,10},{10,... | collective-permute-start | bytes 884744 | tf_op jit(solution)/shard_map/ppermute | solution.py:309
  74.6 13.4 %copy-start.12 = (bf16[128,1152]{1,0:T(8,128)(2,1)}, bf16[128,1152]{1,0:T(8,128)(2,1)S(1)}, u32[]{:S(2)}) copy-start(bf16[128,1152]{1,0:T(8,128)(2,1)S(1)} %collective-permute-done.5.refs_2_) | copy-start | bytes 884740
  81.0 7.0 %copy-start.13 = (bf16[128,1152]{1,0:T(8,128)(2,1)}, bf16[128,1152]{1,0:T(8,128)(2,1)S(1)}, u32[]{:S(2)}) copy-start(bf16[128,1152]{1,0:T(8,128)(2,1)S(1)} %collective-permute-done.6.refs_3_) | copy-start | bytes 884740
  88.0 0.7 copy-start.14
  105.6 1.1 copy-start.9
  105.6 33.1 %copy-start.3 = (bf16[2,288,1152]{2,1,0:T(8,128)(2,1)S(1)}, bf16[2,288,1152]{2,1,0:T(8,128)(2,1)}, u32[]{:S(2)}) copy-start(bf16[2,288,1152]{2,1,0:T(8,128)(2,1)} %copy-done.2) | copy-start | bytes 3981316
  105.6 33.1 %copy-start.5 = (bf16[2,288,1152]{2,1,0:T(8,128)(2,1)S(1)}, bf16[2,288,1152]{2,1,0:T(8,128)(2,1)}, u32[]{:S(2)}) copy-start(bf16[2,288,1152]{2,1,0:T(8,128)(2,1)} %refs_2_.1) | copy-start | bytes 3981316
  105.6 41.0 %collective-permute-start.10 = (bf16[1152,1152]{1,0:T(8,128)(2,1)}, bf16[1152,1152]{1,0:T(8,128)(2,1)S(1)}, u32[]{:S(2)}, u32[]{:S(2)}) collective-permute-start(bf16[1152,1152]{1,0:T(8,128)(2,1)} %shard_map.79.refs_2_), channel_id=1, source_target_pairs={{0,1},{1,0},{2,3},{3,2},{4,5},{5,4},{6,7},{7,6},{8,9},{9,8},{10,11... | collective-permute-start | bytes 7962632 | tf_op jit(solution)/shard_map/ppermute | solution.py:309
  138.8 7.9 %copy-start = (bf16[1152,1152]{1,0:T(8,128)(2,1)S(1)}, bf16[1152,1152]{1,0:T(8,128)(2,1)}, u32[]{:S(2)}) copy-start(bf16[1152,1152]{1,0:T(8,128)(2,1)} %shard_map.79.refs_2_) | copy-start | bytes 7962628
  177.1 2.4 %copy-start.1 = (bf16[64,4,1152]{2,1,0:T(4,128)(2,1)S(1)}, bf16[64,4,1152]{2,1,0:T(4,128)(2,1)}, u32[]{:S(2)}) copy-start(bf16[64,4,1152]{2,1,0:T(4,128)(2,1)} %all_to_all.11.refs_1_.in_b) | copy-start | bytes 1769476
  177.1 2.4 %copy-start.4 = (f32[4,64,1152]{2,1,0:T(8,128)S(1)}, f32[4,64,1152]{2,1,0:T(8,128)}, u32[]{:S(2)}) copy-start(f32[4,64,1152]{2,1,0:T(8,128)} %get-tuple-element.25.refs_1_.in_a) | copy-start | bytes 3538948
  177.1 2.4 %copy-start.6 = (f32[3,3,1152]{2,1,0:T(4,128)S(1)}, f32[3,3,1152]{2,1,0:T(4,128)}, u32[]{:S(2)}) copy-start(f32[3,3,1152]{2,1,0:T(4,128)} %mod_ref.7) | copy-start | bytes 124420
  177.4 11.3 %collective-permute-start.12 = (bf16[2304,1152]{1,0:T(8,128)(2,1)}, bf16[2304,1152]{1,0:T(8,128)(2,1)S(1)}, u32[]{:S(2)}, u32[]{:S(2)}) collective-permute-start(bf16[2304,1152]{1,0:T(8,128)(2,1)} %shard_map.82.refs_4_), channel_id=1, source_target_pairs={{0,1},{1,0},{2,3},{3,2},{4,5},{5,4},{6,7},{7,6},{8,9},{9,8},{10,11... | collective-permute-start | bytes 15925256 | tf_op jit(solution)/shard_map/ppermute | solution.py:309
Sparse Core Ops, SparseCore 0:
  41.6 64.0 all-gather.2
  108.1 69.2 all-gather.4

commit v2 on v1

--- a/solution.py
+++ b/solution.py
@@ -222,6 +222,9 @@
         scratch_shapes=[pltpu.VMEM(latents.shape, F32)]
         + [pltpu.VMEM(part.shape, BF) for part in back]
         + [pltpu.SemaphoreType.DMA((5,)), pltpu.VMEM(latents.shape, F32)],
+        cost_estimate=pl.CostEstimate(
+            flops=10**11, bytes_accessed=8 * latents.size, transcendentals=0
+        ),
         compiler_params=pltpu.CompilerParams(vmem_limit_bytes=62 * 2**20),
     )(core.reshape(1), time_embed, modulation, latents, *back)
 
@@ -239,7 +242,7 @@
         pltpu.make_async_copy(in_b, held_b, in_sems.at[1]),
     ]
     copies = [pltpu.make_async_copy(b, held.at[i], sems.at[i]) for i, b in enumerate(blocks)]
-    for copy in arrivals + copies[:2]:
+    for copy in arrivals + copies[:3]:
         copy.start()
     arrivals[0].wait()
     if first:
@@ -257,13 +260,13 @@
     total = None
     for k in range(0, len(blocks), 2):
         copies[k].wait()
-        if k + 2 < len(blocks):
-            copies[k + 2].start()
+        if k + 3 < len(blocks):
+            copies[k + 3].start()
         v = dot(x, held[k], 1, 0)
         inner = 0.5 * v * (1.0 + jnp.tanh(math.sqrt(2.0 / math.pi) * (v + 0.044715 * (v * v * v))))
         copies[k + 1].wait()
-        if k + 3 < len(blocks):
-            copies[k + 3].start()
+        if k + 4 < len(blocks):
+            copies[k + 4].start()
         part = dot(inner.astype(BF), held[k + 1], 1, 0)
         total = part if total is None else total + part
     if first:

time: 200 us -> 198 us (0.990)
    all_gather x2, waiting for transfers between devices: 12.2 us -> 14.6 us  [gather(): lax.all_gather(piece, 'seq', axis=0, tiled=True, axis_index_groups=PLANE)]
  transfers between devices with their start and end apart: 15 -> 15, of which waited for: 6 -> 6; matrix products, arithmetic and copies ran while one was open for 2% -> 2% of each run, Pallas kernels for 22% -> 21%
where the time goes in v2:
time: 198 us
  blocking collectives  54.3 us (27%)
  Pallas kernels  46.8 us (24%)
  waiting for transfers between devices  42.2 us (21%)
  starting transfers between devices  33.7 us (17%)
  between operations  13.6 us (7%)
  local copies, waits for them, and re-layouts  3.71 us (2%)
  other arithmetic  3.59 us (2%)
    all_to_all x2, blocking collectives, regroup(): return lax.all_to_all(rows, 'seq', split_axis=0, concat_axis=0, tiled=True)  54.3 us
    ppermute x13, starting transfers between devices, swap(): return lax.ppermute(x, 'tp', SWAPS[d])  33.7 us
    ppermute x13, waiting for transfers between devices, swap(): return lax.ppermute(x, 'tp', SWAPS[d])  27.6 us
    pallas_call x3, Pallas kernels, attend(): pl.pallas_call(functools.partial(attend_kernel, pieces, len(inits), layer...  26 us
    all_gather x2, waiting for transfers between devices, gather(): lax.all_gather(piece, 'seq', axis=0, tiled=True, axis_index_groups=PLANE)  14.6 us
    pallas_call x2, Pallas kernels, mlp(): pl.pallas_call(functools.partial(mlp_kernel, first, len(weights)), out_sh...  13.1 us
    pallas_call x1, Pallas kernels, finish_spatial(): pl.pallas_call(middle_kernel, out_shape=[jax.ShapeDtypeStruct((frames, lo...  4.78 us
  transfers between devices with their start and end apart: 15, of which 6 were waited for; matrix products, arithmetic and copies ran while one was open for 2% of the time, Pallas kernels for 21%

profile of v2, /device:TPU:1, one launch (start us, length us, event | category | flops | bytes accessed | tf_op | source)
XLA Modules:
  0.0 197.9 jit_solution(1757584058082969928)
XLA Ops:
  6.5 3.2 %collective-permute-start = (bf16[2,864,1152]{2,1,0:T(8,128)(2,1)}, bf16[2,864,1152]{2,1,0:T(8,128)(2,1)}, u32[]{:S(2)}, u32[]{:S(2)}) collective-permute-start(bf16[2,864,1152]{2,1,0:T(8,128)(2,1)} %bitcast.6), channel_id=1, source_target_pairs={{0,1},{1,0},{2,3},{3,2},{4,5},{5,4},{6,7},{7,6},{8,9},{9,8},{10,11... | collective-permute-start | bytes 11943944 | tf_op jit(solution)/shard_map/ppermute | solution.py:312
  9.8 0.0 collective-permute-start.1
  9.8 1.7 select_bitcast_fusion.piece_ref
  11.5 2.9 %shard_map.73 = (bf16[128,1152]{1,0:T(8,128)(2,1)}, bf16[128,1152]{1,0:T(8,128)(2,1)}, bf16[200,1152]{1,0:T(8,128)(2,1)}) custom-call(s32[1]{0:T(128)} %bitcast.core_ref, f32[64,4,1152]{2,1,0:T(4,128)} %refs_0_.2, f32[3,3,1152]{2,1,0:T(4,128)} %mod_ref.7, bf16[72,1152]{1,0:T(8,128)(2,1)} %select_bitcast_fusion.piece_ref), custom_call_target="tpu_custom_call" | custom-call | tf_op jit(solution)/shard_map/pallas_call | solution.py:177
  14.4 5.2 %collective-permute-start.3 = (bf16[200,1152]{1,0:T(8,128)(2,1)}, bf16[200,1152]{1,0:T(8,128)(2,1)S(1)}, u32[]{:S(2)}, u32[]{:S(2)}) collective-permute-start(bf16[200,1152]{1,0:T(8,128)(2,1)} %get-tuple-element.20), channel_id=1, source_target_pairs={{0,2},{1,3},{2,0},{3,1},{4,6},{5,7},{6,4},{7,5},{8,10},{9,11},{10,... | collective-permute-start | bytes 1382408 | tf_op jit(solution)/shard_map/ppermute | solution.py:312
  19.6 1.9 dynamic-slice_select_fusion.refs_3_
  21.5 0.0 collective-permute-done.1.refs_2_.refs_7_.refs_4_
  21.5 0.0 collective-permute-done.refs_1_.refs_6_.refs_3_
  21.5 1.1 copy-done.2
  22.5 0.8 collective-permute-start.2
  23.3 1.6 collective-permute-start.4
  24.9 7.4 %collective-permute-done.3.refs_2_ = bf16[200,1152]{1,0:T(8,128)(2,1)S(1)} collective-permute-done((bf16[200,1152]{1,0:T(8,128)(2,1)}, bf16[200,1152]{1,0:T(8,128)(2,1)S(1)}, u32[]{:S(2)}, u32[]{:S(2)}) %collective-permute-start.3) | collective-permute-done | bytes 460832 | tf_op jit(solution)/shard_map/ppermute | solution.py:312
  32.3 0.7 slice.4.refs_0_
  33.0 0.0 collective-permute-done.2.refs_1_
  33.0 7.7 %collective-permute-done.4.refs_3_.refs_2_ = bf16[128,1152]{1,0:T(8,128)(2,1)S(1)} collective-permute-done((bf16[128,1152]{1,0:T(8,128)(2,1)}, bf16[128,1152]{1,0:T(8,128)(2,1)S(1)}, u32[]{:S(2)}, u32[]{:S(2)}) %collective-permute-start.4) | collective-permute-done | bytes 294944 | tf_op jit(solution)/shard_map/ppermute | solution.py:312
  40.7 0.7 copy-done.11
  41.4 0.0 all-gather.3.cloned.1.call-update
  41.4 0.0 all-gather.5.cloned.1.call-start
  41.5 13.9 %collective-permute-start.11 = (bf16[144,1152]{1,0:T(8,128)(2,1)S(1)}, bf16[144,1152]{1,0:T(8,128)(2,1)S(1)}, u32[]{:S(2)}, u32[]{:S(2)}) collective-permute-start(bf16[144,1152]{1,0:T(8,128)(2,1)S(1)} %copy-done.8), channel_id=1, source_target_pairs={{0,2},{1,3},{2,0},{3,1},{4,6},{5,7},{6,4},{7,5},{8,10},{9,11},{10,... | collective-permute-start | bytes 995336 | tf_op jit(solution)/shard_map/ppermute | solution.py:312
  55.3 11.8 %shard_map.75 = (bf16[128,1152]{1,0:T(8,128)(2,1)}, bf16[128,1152]{1,0:T(8,128)(2,1)}, bf16[128,1152]{1,0:T(8,128)(2,1)}, bf16[128,1152]{1,0:T(8,128)(2,1)}) custom-call(bf16[128,1152]{1,0:T(8,128)(2,1)} %get-tuple-element.18.refs_0_, bf16[128,1152]{1,0:T(8,128)(2,1)} %copy-done.10, bf16[200,1152]{1,0:T(8,128)(2,1)} %copy-done.12, ...), custom_call_target="tpu_custom_call" | custom-call | flops 4076863488 | bytes 5308416 | tf_op jit(solution)/shard_map/pallas_call | solution.py:128
  67.2 0.1 collective-permute-start.5
  67.3 0.1 collective-permute-start.6
  67.4 5.9 %collective-permute-start.7 = (bf16[128,1152]{1,0:T(8,128)(2,1)}, bf16[128,1152]{1,0:T(8,128)(2,1)S(1)}, u32[]{:S(2)}, u32[]{:S(2)}) collective-permute-start(bf16[128,1152]{1,0:T(8,128)(2,1)} %get-tuple-element.24), channel_id=1, source_target_pairs={{0,3},{1,2},{2,1},{3,0},{4,7},{5,6},{6,5},{7,4},{8,11},{9,10},{10,... | collective-permute-start | bytes 884744 | tf_op jit(solution)/shard_map/ppermute | solution.py:312
  73.3 0.0 collective-permute-start.8
  73.3 0.0 collective-permute-done.11.refs_0_
  73.3 0.5 collective-permute-start.9
  73.8 0.2 copy-done.7
  74.1 0.0 all-gather.5.cloned.1.call-update
  74.1 0.0 collective-permute-done.5.refs_2_
  74.1 5.6 %collective-permute-done.6.refs_3_ = bf16[128,1152]{1,0:T(8,128)(2,1)S(1)} collective-permute-done((bf16[128,1152]{1,0:T(8,128)(2,1)}, bf16[128,1152]{1,0:T(8,128)(2,1)S(1)}, u32[]{:S(2)}, u32[]{:S(2)}) %collective-permute-start.6) | collective-permute-done | bytes 294944 | tf_op jit(solution)/shard_map/ppermute | solution.py:312
  79.7 6.9 %collective-permute-done.7.refs_4_ = bf16[128,1152]{1,0:T(8,128)(2,1)S(1)} collective-permute-done((bf16[128,1152]{1,0:T(8,128)(2,1)}, bf16[128,1152]{1,0:T(8,128)(2,1)S(1)}, u32[]{:S(2)}, u32[]{:S(2)}) %collective-permute-start.7) | collective-permute-done | bytes 294944 | tf_op jit(solution)/shard_map/ppermute | solution.py:312
  86.7 0.7 copy-done.15
  87.4 4.8 %shard_map.76 = (f32[4,64,1152]{2,1,0:T(8,128)}, bf16[64,4,1152]{2,1,0:T(4,128)(2,1)}) custom-call(s32[1]{0:T(128)} %bitcast.core_ref, f32[4,1152]{1,0:T(4,128)} %embed_ref.1, f32[3,3,1152]{2,1,0:T(4,128)} %mod_ref.7, f32[64,4,1152]{2,1,0:T(4,128)} %refs_0_.2, bf16[128,1152]{1,0:T(8,128)(2,1)} %get-tuple-element.21.refs_1_, bf16[128,1152]{1,0:T(8,128)(2,1)} %copy-done.13, ...), custom_call_target="tpu_custom_call" | custom-call | flops 99999997952 | bytes 2359296 | tf_op jit(solution)/shard_map/pallas_call | solution.py:212
  92.2 0.0 collective-permute-done.9.refs_3_
  92.2 13.4 %all-gather.3.cloned.1.call-done.refs_0_ = bf16[1152,1152]{1,0:T(8,128)(2,1)} async-done(((bf16[72,1152]{1,0:T(8,128)(2,1)}), bf16[1152,1152]{1,0:T(8,128)(2,1)}) %all-gather.3.cloned.1.call-update) | async-done | bytes 2654224 | tf_op jit(solution)/shard_map/all_gather | solution.py:316
  105.6 1.0 collective-permute-start.10
  106.6 0.1 copy-done.9
  106.7 30.2 %all_to_all.10.refs_0_ = bf16[64,4,1152]{2,1,0:T(4,128)(2,1)S(1)} all-to-all(bf16[64,4,1152]{2,1,0:T(4,128)(2,1)S(1)} %copy-done.9), channel_id=1, replica_groups=mesh['seq'=64,'tp'=4] {'seq'}, dimensions={0} | all-to-all | bytes 1179648 | tf_op jit(solution)/shard_map/all_to_all | solution.py:374
  136.8 7.9 %shard_map.77 = (f32[256,1152]{1,0:T(8,128)S(1)}, bf16[256,1152]{1,0:T(8,128)(2,1)S(1)}) custom-call(bf16[64,4,1152]{2,1,0:T(4,128)(2,1)S(1)} %all_to_all.10.refs_0_, bf16[2,864,1152]{2,1,0:T(8,128)(2,1)} %bitcast.9, bf16[2,288,1152]{2,1,0:T(8,128)(2,1)S(1)} %copy-done.5, bf16[2,864,1152]{2,1,0:T(8,128)(2,1)} %collective-permute-done.refs_1_.refs_6_.refs_3_, ...), custom_call_target="tpu_custom_call" | custom-call | flops 2038431744 | bytes 5308416 | tf_op jit(solution)/shard_map/pallas_call | solution.py:128
  144.7 0.0 collective-permute-done.10.refs_3_
  144.8 6.3 %shard_map.80 = bf16[64,4608]{1,0:T(8,128)(2,1)S(1)} custom-call(bf16[256,1152]{1,0:T(8,128)(2,1)S(1)} %get-tuple-element.27.refs_0_, f32[256,1152]{1,0:T(8,128)S(1)} %get-tuple-element.28.refs_1_, bf16[1152,1152]{1,0:T(8,128)(2,1)S(1)} %copy-done, bf16[1152,1152]{1,0:T(8,128)(2,1)S(1)} %collective-permute-done.10.refs_3_), custom_call_target="tpu_custom_call" | custom-call | flops 2038431744 | bytes 5308416 | tf_op jit(solution)/shard_map/pallas_call | solution.py:128
  151.1 0.1 reshape.14
  151.2 24.1 %all_to_all.11.refs_1_.in_b = bf16[64,4,1152]{2,1,0:T(4,128)(2,1)} all-to-all(bf16[64,4,1152]{2,1,0:T(4,128)(2,1)S(1)} %reshape.14), channel_id=1, replica_groups=mesh['seq'=64,'tp'=4] {'seq'}, dimensions={0} | all-to-all | bytes 1179648 | tf_op jit(solution)/shard_map/all_to_all | solution.py:374
  175.4 1.1 all-gather.5.cloned.1.call-done.refs_0_
  176.5 1.4 collective-permute-start.12
  177.9 8.8 %shard_map.83 = (f32[256,1152]{1,0:T(8,128)S(1)}, bf16[256,1152]{1,0:T(8,128)(2,1)S(1)}) custom-call(f32[3,3,1152]{2,1,0:T(4,128)S(1)} %copy-done.6, f32[4,64,1152]{2,1,0:T(8,128)S(1)} %copy-done.4, bf16[64,4,1152]{2,1,0:T(4,128)(2,1)S(1)} %copy-done.1, bf16[1152,1152]{1,0:T(8,128)(2,1)} %refs_0_.3, bf16[1152,1152]{1,0:T(8,128)(2,1)} %refs_1_.1, ...), custom_call_target="tpu_custom_call" | custom-call | flops 4076863488 | bytes 15925248 | tf_op jit(solution)/shard_map/pallas_call | solution.py:289
  186.7 0.0 collective-permute-done.12.refs_0_
  186.7 4.3 %shard_map.84 = f32[64,4,1152]{2,1,0:T(4,128)} custom-call(f32[3,3,1152]{2,1,0:T(4,128)S(1)} %copy-done.6, bf16[256,1152]{1,0:T(8,128)(2,1)S(1)} %get-tuple-element.29.in_a, f32[256,1152]{1,0:T(8,128)S(1)} %get-tuple-element.30.in_b, bf16[2304,1152]{1,0:T(8,128)(2,1)S(1)} %collective-permute-done.12.refs_0_), custom_call_target="tpu_custom_call" | custom-call | flops 1358954496 | bytes 5308416 | tf_op jit(solution)/shard_map/pallas_call | solution.py:289
  (34 shorter events, 0.1 us)
Async XLA Ops:
  6.5 99.1 %all-gather.3.cloned.1.call-start = ((), (), s32[]{:S(2)}) async-start(), calls=%async_computation.2 | async-start | bytes 2820096 | tf_op jit(solution)/shard_map/all_gather | solution.py:316
  6.5 14.9 %collective-permute-start = (bf16[2,864,1152]{2,1,0:T(8,128)(2,1)}, bf16[2,864,1152]{2,1,0:T(8,128)(2,1)}, u32[]{:S(2)}, u32[]{:S(2)}) collective-permute-start(bf16[2,864,1152]{2,1,0:T(8,128)(2,1)} %bitcast.6), channel_id=1, source_target_pairs={{0,1},{1,0},{2,3},{3,2},{4,5},{5,4},{6,7},{7,6},{8,9},{9,8},{10,11... | collective-permute-start | bytes 11943944 | tf_op jit(solution)/shard_map/ppermute | solution.py:312
  9.8 11.7 %collective-permute-start.1 = (bf16[2,288,1152]{2,1,0:T(8,128)(2,1)}, bf16[2,288,1152]{2,1,0:T(8,128)(2,1)S(1)}, u32[]{:S(2)}, u32[]{:S(2)}) collective-permute-start(bf16[2,288,1152]{2,1,0:T(8,128)(2,1)} %refs_2_.1), channel_id=1, source_target_pairs={{0,1},{1,0},{2,3},{3,2},{4,5},{5,4},{6,7},{7,6},{8,9},{9,8},{10,11... | collective-permute-start | bytes 3981320 | tf_op jit(solution)/shard_map/ppermute | solution.py:312
  14.4 17.9 %collective-permute-start.3 = (bf16[200,1152]{1,0:T(8,128)(2,1)}, bf16[200,1152]{1,0:T(8,128)(2,1)S(1)}, u32[]{:S(2)}, u32[]{:S(2)}) collective-permute-start(bf16[200,1152]{1,0:T(8,128)(2,1)} %get-tuple-element.20), channel_id=1, source_target_pairs={{0,2},{1,3},{2,0},{3,1},{4,6},{5,7},{6,4},{7,5},{8,10},{9,11},{10,... | collective-permute-start | bytes 1382408 | tf_op jit(solution)/shard_map/ppermute | solution.py:312
  21.5 1.1 copy-start.2
  22.5 18.9 %copy-start.8 = (bf16[144,1152]{1,0:T(8,128)(2,1)S(1)}, bf16[144,1152]{1,0:T(8,128)(2,1)}, u32[]{:S(2)}) copy-start(bf16[144,1152]{1,0:T(8,128)(2,1)} %dynamic-slice_select_fusion.refs_3_) | copy-start | bytes 995332
  22.5 10.4 %collective-permute-start.2 = (bf16[128,1152]{1,0:T(8,128)(2,1)}, bf16[128,1152]{1,0:T(8,128)(2,1)S(1)}, u32[]{:S(2)}, u32[]{:S(2)}) collective-permute-start(bf16[128,1152]{1,0:T(8,128)(2,1)} %shard_map.74), channel_id=1, source_target_pairs={{0,1},{1,0},{2,3},{3,2},{4,5},{5,4},{6,7},{7,6},{8,9},{9,8},{10,11... | collective-permute-start | bytes 884744 | tf_op jit(solution)/shard_map/ppermute | solution.py:312
  23.3 17.3 %collective-permute-start.4 = (bf16[128,1152]{1,0:T(8,128)(2,1)}, bf16[128,1152]{1,0:T(8,128)(2,1)S(1)}, u32[]{:S(2)}, u32[]{:S(2)}) collective-permute-start(bf16[128,1152]{1,0:T(8,128)(2,1)} %shard_map.74), channel_id=1, source_target_pairs={{0,3},{1,2},{2,1},{3,0},{4,7},{5,6},{6,5},{7,4},{8,11},{9,10},{10,... | collective-permute-start | bytes 884744 | tf_op jit(solution)/shard_map/ppermute | solution.py:312
  32.3 23.1 %copy-start.12 = (bf16[200,1152]{1,0:T(8,128)(2,1)}, bf16[200,1152]{1,0:T(8,128)(2,1)S(1)}, u32[]{:S(2)}) copy-start(bf16[200,1152]{1,0:T(8,128)(2,1)S(1)} %collective-permute-done.3.refs_2_) | copy-start | bytes 1382404
  33.0 7.7 %copy-start.10 = (bf16[128,1152]{1,0:T(8,128)(2,1)}, bf16[128,1152]{1,0:T(8,128)(2,1)S(1)}, u32[]{:S(2)}) copy-start(bf16[128,1152]{1,0:T(8,128)(2,1)S(1)} %collective-permute-done.2.refs_1_) | copy-start | bytes 884740
  40.7 0.7 copy-start.11
  41.4 135.1 %all-gather.5.cloned.1.call-start = ((), (), s32[]{:S(2)}) async-start(), calls=%async_computation.3 | async-start | bytes 5640192 | tf_op jit(solution)/shard_map/all_gather | solution.py:316
  41.5 31.8 %collective-permute-start.11 = (bf16[144,1152]{1,0:T(8,128)(2,1)S(1)}, bf16[144,1152]{1,0:T(8,128)(2,1)S(1)}, u32[]{:S(2)}, u32[]{:S(2)}) collective-permute-start(bf16[144,1152]{1,0:T(8,128)(2,1)S(1)} %copy-done.8), channel_id=1, source_target_pairs={{0,2},{1,3},{2,0},{3,1},{4,6},{5,7},{6,4},{7,5},{8,10},{9,11},{10,... | collective-permute-start | bytes 995336 | tf_op jit(solution)/shard_map/ppermute | solution.py:312
  67.2 6.9 %collective-permute-start.5 = (bf16[128,1152]{1,0:T(8,128)(2,1)}, bf16[128,1152]{1,0:T(8,128)(2,1)S(1)}, u32[]{:S(2)}, u32[]{:S(2)}) collective-permute-start(bf16[128,1152]{1,0:T(8,128)(2,1)} %get-tuple-element.22), channel_id=1, source_target_pairs={{0,1},{1,0},{2,3},{3,2},{4,5},{5,4},{6,7},{7,6},{8,9},{9,8},{10,11... | collective-permute-start | bytes 884744 | tf_op jit(solution)/shard_map/ppermute | solution.py:312
  67.3 12.5 %collective-permute-start.6 = (bf16[128,1152]{1,0:T(8,128)(2,1)}, bf16[128,1152]{1,0:T(8,128)(2,1)S(1)}, u32[]{:S(2)}, u32[]{:S(2)}) collective-permute-start(bf16[128,1152]{1,0:T(8,128)(2,1)} %get-tuple-element.23), channel_id=1, source_target_pairs={{0,2},{1,3},{2,0},{3,1},{4,6},{5,7},{6,4},{7,5},{8,10},{9,11},{10,... | collective-permute-start | bytes 884744 | tf_op jit(solution)/shard_map/ppermute | solution.py:312
  67.4 19.3 %collective-permute-start.7 = (bf16[128,1152]{1,0:T(8,128)(2,1)}, bf16[128,1152]{1,0:T(8,128)(2,1)S(1)}, u32[]{:S(2)}, u32[]{:S(2)}) collective-permute-start(bf16[128,1152]{1,0:T(8,128)(2,1)} %get-tuple-element.24), channel_id=1, source_target_pairs={{0,3},{1,2},{2,1},{3,0},{4,7},{5,6},{6,5},{7,4},{8,11},{9,10},{10,... | collective-permute-start | bytes 884744 | tf_op jit(solution)/shard_map/ppermute | solution.py:312
  73.3 18.9 %collective-permute-start.8 = (bf16[1152,1152]{1,0:T(8,128)(2,1)}, bf16[1152,1152]{1,0:T(8,128)(2,1)}, u32[]{:S(2)}, u32[]{:S(2)}) collective-permute-start(bf16[1152,1152]{1,0:T(8,128)(2,1)} %refs_0_.3), channel_id=1, source_target_pairs={{0,1},{1,0},{2,3},{3,2},{4,5},{5,4},{6,7},{7,6},{8,9},{9,8},{10,11... | collective-permute-start | bytes 7962632 | tf_op jit(solution)/shard_map/ppermute | solution.py:312
  73.3 0.7 copy-start.7
  73.3 18.9 %collective-permute-start.9 = (bf16[1152,1152]{1,0:T(8,128)(2,1)}, bf16[1152,1152]{1,0:T(8,128)(2,1)}, u32[]{:S(2)}, u32[]{:S(2)}) collective-permute-start(bf16[1152,1152]{1,0:T(8,128)(2,1)} %refs_1_.1), channel_id=1, source_target_pairs={{0,1},{1,0},{2,3},{3,2},{4,5},{5,4},{6,7},{7,6},{8,9},{9,8},{10,11... | collective-permute-start | bytes 7962632 | tf_op jit(solution)/shard_map/ppermute | solution.py:312
  74.1 12.6 %copy-start.13 = (bf16[128,1152]{1,0:T(8,128)(2,1)}, bf16[128,1152]{1,0:T(8,128)(2,1)S(1)}, u32[]{:S(2)}) copy-start(bf16[128,1152]{1,0:T(8,128)(2,1)S(1)} %collective-permute-done.5.refs_2_) | copy-start | bytes 884740
  79.7 6.9 %copy-start.14 = (bf16[128,1152]{1,0:T(8,128)(2,1)}, bf16[128,1152]{1,0:T(8,128)(2,1)S(1)}, u32[]{:S(2)}) copy-start(bf16[128,1152]{1,0:T(8,128)(2,1)S(1)} %collective-permute-done.6.refs_3_) | copy-start | bytes 884740
  86.7 0.7 copy-start.15
  105.6 1.1 copy-start.9
  105.6 31.2 %copy-start.3 = (bf16[2,288,1152]{2,1,0:T(8,128)(2,1)S(1)}, bf16[2,288,1152]{2,1,0:T(8,128)(2,1)}, u32[]{:S(2)}) copy-start(bf16[2,288,1152]{2,1,0:T(8,128)(2,1)} %copy-done.2) | copy-start | bytes 3981316
  105.6 31.2 %copy-start.5 = (bf16[2,288,1152]{2,1,0:T(8,128)(2,1)S(1)}, bf16[2,288,1152]{2,1,0:T(8,128)(2,1)}, u32[]{:S(2)}) copy-start(bf16[2,288,1152]{2,1,0:T(8,128)(2,1)} %refs_2_.1) | copy-start | bytes 3981316
  105.6 39.1 %collective-permute-start.10 = (bf16[1152,1152]{1,0:T(8,128)(2,1)}, bf16[1152,1152]{1,0:T(8,128)(2,1)S(1)}, u32[]{:S(2)}, u32[]{:S(2)}) collective-permute-start(bf16[1152,1152]{1,0:T(8,128)(2,1)} %shard_map.79.refs_2_), channel_id=1, source_target_pairs={{0,1},{1,0},{2,3},{3,2},{4,5},{5,4},{6,7},{7,6},{8,9},{9,8},{10,11... | collective-permute-start | bytes 7962632 | tf_op jit(solution)/shard_map/ppermute | solution.py:312
  136.8 7.9 %copy-start = (bf16[1152,1152]{1,0:T(8,128)(2,1)S(1)}, bf16[1152,1152]{1,0:T(8,128)(2,1)}, u32[]{:S(2)}) copy-start(bf16[1152,1152]{1,0:T(8,128)(2,1)} %shard_map.79.refs_2_) | copy-start | bytes 7962628
  175.4 2.5 %copy-start.1 = (bf16[64,4,1152]{2,1,0:T(4,128)(2,1)S(1)}, bf16[64,4,1152]{2,1,0:T(4,128)(2,1)}, u32[]{:S(2)}) copy-start(bf16[64,4,1152]{2,1,0:T(4,128)(2,1)} %all_to_all.11.refs_1_.in_b) | copy-start | bytes 1769476
  175.4 2.5 %copy-start.4 = (f32[4,64,1152]{2,1,0:T(8,128)S(1)}, f32[4,64,1152]{2,1,0:T(8,128)}, u32[]{:S(2)}) copy-start(f32[4,64,1152]{2,1,0:T(8,128)} %get-tuple-element.25.refs_1_.in_a) | copy-start | bytes 3538948
  175.4 2.5 %copy-start.6 = (f32[3,3,1152]{2,1,0:T(4,128)S(1)}, f32[3,3,1152]{2,1,0:T(4,128)}, u32[]{:S(2)}) copy-start(f32[3,3,1152]{2,1,0:T(4,128)} %mod_ref.7) | copy-start | bytes 124420
  176.5 10.2 %collective-permute-start.12 = (bf16[2304,1152]{1,0:T(8,128)(2,1)}, bf16[2304,1152]{1,0:T(8,128)(2,1)S(1)}, u32[]{:S(2)}, u32[]{:S(2)}) collective-permute-start(bf16[2304,1152]{1,0:T(8,128)(2,1)} %shard_map.82.refs_4_), channel_id=1, source_target_pairs={{0,1},{1,0},{2,3},{3,2},{4,5},{5,4},{6,7},{7,6},{8,9},{9,8},{10,11... | collective-permute-start | bytes 15925256 | tf_op jit(solution)/shard_map/ppermute | solution.py:312
Sparse Core Ops, SparseCore 0:
  41.5 64.0 all-gather.2
  108.1 68.3 all-gather.4
